TPU v7x, 32 devices: a whole 2x2x4 slice. The times are simulated.
32 devices in a mesh: seq: 16 (over z, y, core), head: 2 (over x).
Axes of the slice: x: 2, y: 2, z: 4, core: 2. Of those that a mesh axis runs over, the one named last changes fastest.
Arguments:
- att_q: bfloat16 [4096, 1280], P('seq', 'head'), may hold values from -150 to 150
- att_k: bfloat16 [4096, 1280], P('seq', 'head'), may hold values from -6 to 6
- att_v: bfloat16 [4096, 1280], P('seq', 'head'), may hold values from -6 to 6
- fast_q: bfloat16 [4096, 1280], P('seq', 'head'), may hold values from -6 to 6
- fast_k: bfloat16 [4096, 1280], P('seq', 'head'), may hold values from -6 to 6
- fast_v: bfloat16 [4096, 1280], P('seq', 'head'), may hold values from -6 to 6
- learn_rates: float32 [4096], P('seq'), may hold values from 0.0002 to 0.002
- w_gate: bfloat16 [640, 1280], P(None, 'head'), may hold values from -0.25 to 0.25
- w_up: bfloat16 [640, 1280], P(None, 'head'), may hold values from -0.25 to 0.25
- w_down: bfloat16 [640, 1280], P(None, 'head'), may hold values from -0.25 to 0.25
Outputs:
- attended: bfloat16 [4096, 1280], P('seq', 'head')
- fast_out: bfloat16 [4096, 1280], P('seq', 'head')
All inputs are finite; a program needn't handle non-finite values.
Results may differ from a plain program's by a relative error of at most 0.007.
The roundings to bfloat16 on the way count: a program that leaves them out, or rounds other values in their place, can miss the bound.
Values may be sent and summed in bfloat16 or wider, within the bound.
No kernel may reach another device: no remote copies, remote signals or barrier semaphores. Data moves between devices by JAX's collectives and lax.ppermute only.
A program may use at most 64 MiB of HBM per device.

v0:
```python
import functools
import math

import jax
import jax.numpy as jnp
from jax import lax
from jax.experimental import pallas as pl
from jax.experimental.pallas import tpu as pltpu
from jax.sharding import PartitionSpec as P

WINDOW = 1024
HEAD_DIM = 128
norm_eps = 1e-06
f32 = jnp.float32
bf16 = jnp.bfloat16

SMEM = pl.BlockSpec(memory_space=pltpu.SMEM)
VMEM = pl.BlockSpec(memory_space=pltpu.VMEM)
HBM = pl.BlockSpec(memory_space=pltpu.HBM)
ANY = pl.BlockSpec(memory_space=pl.ANY)
PARAMS = pltpu.CompilerParams(vmem_limit_bytes=16 << 20)


def swapped(value, bit):
    count = lax.axis_size("seq")
    return lax.ppermute(value, "seq", [(at, at ^ bit) for at in range(count)])


def cost(flops, moved_bytes, exps=0):
    return pl.CostEstimate(flops=flops, bytes_accessed=moved_bytes, transcendentals=exps)


def attention_kernel(place_ref, q_ref, own_ref, back2_ref, back4_ref, pair_ref, out_ref):
    rows, width = q_ref.shape
    place = place_ref[0]
    factor = HEAD_DIM ** (-0.5) * math.log2(math.e)
    q_at = lax.broadcasted_iota(jnp.int32, (rows, rows), 0)
    k_at = lax.broadcasted_iota(jnp.int32, (rows, rows), 1)
    inside = k_at <= q_at

    def attend(cols, masked):
        query = q_ref[:, cols]

        def score(ref, *at):
            return lax.dot_general(
                query, ref[(*at, 0, slice(None), cols)], (((1,), (1,)), ((), ())),
                preferred_element_type=f32,
            )

        def seen(part, back):
            return jnp.where(place >= back, part, -1e30) if masked else part

        parts = [
            jnp.where(inside, score(own_ref), seen(score(back4_ref), 4)),
            seen(score(pair_ref, 0), 1),
            seen(score(back2_ref), 2),
            seen(score(pair_ref, 1), 3),
        ]
        row_max = functools.reduce(
            jnp.maximum, [jnp.max(part, axis=1, keepdims=True) for part in parts]
        )
        shift = row_max * factor
        parts = [jnp.exp2(part * factor - shift) for part in parts]
        total = functools.reduce(jnp.add, [jnp.sum(e, axis=1, keepdims=True) for e in parts])
        scale = 1.0 / total
        parts = [(part * scale).astype(bf16) for part in parts]
        zero = jnp.zeros_like(parts[0])
        parts = [jnp.where(inside, parts[0], zero), jnp.where(inside, zero, parts[0])] + parts[1:]
        result = jnp.zeros((rows, HEAD_DIM), f32)
        for part, ref, at in zip(
            parts, (own_ref, back4_ref, pair_ref, back2_ref, pair_ref), ((), (), (0,), (), (1,))
        ):
            result += jnp.dot(
                part, ref[(*at, 1, slice(None), cols)], preferred_element_type=f32
            )
        out_ref[:, cols] = result.astype(bf16)

    def every(masked):
        for head in range(width // HEAD_DIM):
            attend(slice(head * HEAD_DIM, (head + 1) * HEAD_DIM), masked)

    pl.when(place >= 4)(lambda: every(False))
    pl.when(place < 4)(lambda: every(True))


def attention(place, query, own, back2, back4, pair):
    rows, width = query.shape
    return pl.pallas_call(
        attention_kernel,
        out_shape=jax.ShapeDtypeStruct((rows, width), bf16),
        in_specs=[SMEM] + [VMEM] * 5,
        out_specs=VMEM,
        compiler_params=PARAMS,
        cost_estimate=cost(20 * rows * rows * width, 24 * rows * width, 5 * rows * rows * 5),
        name="attention",
    )(place[None], query, own, back2, back4, pair)


def prepare_kernel(place_ref, gate_ref, up_ref, down_ref, out_ref, wide, hold, sems):
    feats, hidden = gate_ref.shape
    half = hidden // 2
    window = hold.shape[0]
    core = place_ref[0] % 2
    low = pl.multiple_of(core * (hidden - window), 128)
    off = pl.multiple_of(core * (half - hidden + window), 64)
    pieces = sems.shape[1]
    step = feats // pieces
    copies = [
        [
            pltpu.make_async_copy(
                ref.at[pl.ds(piece * step, step), pl.ds(low, window)],
                wide.at[at, pl.ds(piece * step, step), :],
                sems.at[at, piece],
            )
            for piece in range(pieces)
        ]
        for at, ref in enumerate((gate_ref, up_ref, down_ref))
    ]
    for group in copies:
        for copy in group:
            copy.start()
    for at, group in enumerate(copies):
        for copy in group:
            copy.wait()
        hold[...] = wide[at].T
        out_ref[at] = hold[pl.ds(off, half), :]


def prepared(place, w_gate, w_up, w_down):
    feats, hidden = w_gate.shape
    half = hidden // 2
    window = -(-half // 128) * 128
    return pl.pallas_call(
        prepare_kernel,
        out_shape=jax.ShapeDtypeStruct((3, half, feats), bf16),
        in_specs=[SMEM] + [HBM] * 3,
        out_specs=VMEM,
        scratch_shapes=[
            pltpu.VMEM((3, feats, window), bf16),
            pltpu.VMEM((window, feats), bf16),
            pltpu.SemaphoreType.DMA((3, feats // 128)),
        ],
        compiler_params=pltpu.CompilerParams(vmem_limit_bytes=60 << 20),
        cost_estimate=cost(0, 9 * feats * hidden),
        name="prepare",
    )(place[None], w_gate, w_up, w_down)


def grad_kernel(
    place_ref, turned_ref, k0_ref, k1_ref, v0_ref, v1_ref, r0_ref, r1_ref, key_ref, val_ref,
    send, keep, own_ref, hold,
):
    own_ref[0] = key_ref[...]
    own_ref[1] = val_ref[...]

    def project(at, rows):
        return lax.dot_general(
            turned_ref[at], rows, (((1,), (1,)), ((), ())), preferred_element_type=f32
        )

    terms = []
    for keys, vals, rate_ref in ((k0_ref, v0_ref, r0_ref), (k1_ref, v1_ref, r1_ref)):
        rate = rate_ref[...]
        pre_gate = project(0, keys[...])
        pre_up = project(1, keys[...])
        back = rate * project(2, vals[...])
        sigmoid_v = jax.nn.sigmoid(pre_gate)
        silu = pre_gate * sigmoid_v
        slope = sigmoid_v * (1.0 + pre_gate * (1.0 - sigmoid_v))
        terms.append(
            (
                (back * pre_up * slope).astype(bf16),
                (back * silu).astype(bf16),
                (rate * silu * pre_up).astype(bf16),
            )
        )
    sources = ((k0_ref, k1_ref), (k0_ref, k1_ref), (v0_ref, v1_ref))
    for at in range(3):
        hold[at] = jnp.dot(
            terms[0][at], sources[at][0][...], preferred_element_type=f32
        ) + jnp.dot(terms[1][at], sources[at][1][...], preferred_element_type=f32)
    quart = send.shape[2]
    row = (place_ref[0] // 2) % 2
    for at in range(3):
        for other in range(2):
            there = pl.multiple_of((2 * (1 - row) + other) * quart, 8)
            here = pl.multiple_of((2 * row + other) * quart, 8)
            send[at, other] = hold[at, pl.ds(there, quart), :].astype(bf16)
            keep[at, other] = hold[at, pl.ds(here, quart), :]


def gradients(place, turned_w, k0, k1, v0, v1, r0, r1, att_k, att_v):
    _, half, feats = turned_w.shape
    rows = k0.shape[0]
    shape = (3, 2, half // 4, feats)
    return pl.pallas_call(
        grad_kernel,
        out_shape=[
            jax.ShapeDtypeStruct(shape, bf16),
            jax.ShapeDtypeStruct(shape, f32),
            jax.ShapeDtypeStruct((2,) + att_k.shape, bf16),
        ],
        in_specs=[SMEM] + [VMEM] * 9,
        out_specs=[VMEM] * 3,
        scratch_shapes=[pltpu.VMEM((3, half, feats), f32)],
        compiler_params=PARAMS,
        cost_estimate=cost(24 * rows * half * feats, 20 * half * feats, 2 * half * rows),
        name="gradients",
    )(place[None], turned_w, k0, k1, v0, v1, r0, r1, att_k, att_v)


def second_kernel(place_ref, keep, got, send, kept):
    row = (place_ref[0] // 4) % 2
    for at in range(3):
        send[at] = (keep[at, 1 - row] + got[at, 1 - row].astype(f32)).astype(bf16)
        kept[at] = keep[at, row] + got[at, row].astype(f32)


def second_sum(place, keep, got):
    shape = keep.shape[:1] + keep.shape[2:]
    return pl.pallas_call(
        second_kernel,
        out_shape=[jax.ShapeDtypeStruct(shape, bf16), jax.ShapeDtypeStruct(shape, f32)],
        in_specs=[SMEM] + [VMEM] * 2,
        out_specs=[VMEM] * 2,
        compiler_params=PARAMS,
        cost_estimate=cost(keep.size * 2, keep.size * 8),
        name="second",
    )(place[None], keep, got)


def third_kernel(keep, got, tied, total, send):
    del tied
    for at in range(3):
        summed = keep[at] + got[at].astype(f32)
        total[at] = summed
        send[at] = summed.astype(bf16)


def third_sum(keep, got, tied):
    return pl.pallas_call(
        third_kernel,
        out_shape=[
            jax.ShapeDtypeStruct(keep.shape, f32),
            jax.ShapeDtypeStruct(keep.shape, bf16),
        ],
        in_specs=[VMEM] * 2 + [ANY],
        out_specs=[VMEM] * 2,
        compiler_params=PARAMS,
        cost_estimate=cost(keep.size * 2, keep.size * 8),
        name="third",
    )(keep, got, tied)


def window_kernel(place_ref, own_ref, back_ref, tied, out_ref):
    del tied
    early = (place_ref[0] // 2) % 2 == 0

    @pl.when(early)
    def _():
        out_ref[...] = own_ref[...]

    @pl.when(jnp.logical_not(early))
    def _():
        out_ref[...] = back_ref[...]


def window_step(place, own, back4, tied):
    return pl.pallas_call(
        window_kernel,
        out_shape=jax.ShapeDtypeStruct(own.shape, bf16),
        in_specs=[SMEM] + [VMEM] * 2 + [ANY],
        out_specs=VMEM,
        compiler_params=PARAMS,
        cost_estimate=cost(0, own.size * 4),
        name="window",
    )(place[None], own, back4, tied)


def renorm_kernel(old_ref, keep, got, part_a, part_b):
    rows = part_a.shape[1]
    for at in range(3):
        old = old_ref[at].astype(f32)
        updated = old + (keep[at] + got[at].astype(f32))
        old_norm = jnp.sqrt(jnp.sum(old * old, axis=1, keepdims=True))
        squares = jnp.sum(updated * updated, axis=1, keepdims=True)
        fresh = updated * (old_norm / jnp.sqrt(squares + norm_eps))
        part_a[at] = fresh[:rows].astype(bf16)
        part_b[at] = fresh[rows:].astype(bf16)


def renormed(old, keep, got):
    part = jax.ShapeDtypeStruct((3, old.shape[1] // 2, old.shape[2]), bf16)
    return pl.pallas_call(
        renorm_kernel,
        out_shape=[part, part],
        in_specs=[VMEM] * 3,
        out_specs=[VMEM] * 2,
        compiler_params=PARAMS,
        cost_estimate=cost(old.size * 8, old.size * 10),
        name="renorm",
    )(old, keep, got)


def near_kernel(
    place_ref, part_a, got_a, part_b, got_b, own_ref, back2_ref, back4_ref,
    near_a, near_b, near, pair,
):
    rows = part_a.shape[1]
    for at in range(3):
        for part, got, out, low in (
            (part_a, got_a, near_a, 0),
            (part_b, got_b, near_b, 2 * rows),
        ):
            both = jnp.concatenate([part[at].astype(f32), got[at].astype(f32)], axis=0)
            out[at] = both.astype(bf16)
            near[at, low : low + 2 * rows] = both.astype(bf16)
    even = place_ref[0] % 2 == 0

    @pl.when(even)
    def _():
        pair[0] = own_ref[...]
        pair[1] = back2_ref[...]

    @pl.when(jnp.logical_not(even))
    def _():
        pair[0] = back2_ref[...]
        pair[1] = back4_ref[...]


def near_rows(place, part_a, got_a, part_b, got_b, own, back2, back4):
    rows, feats = part_a.shape[1:]
    return pl.pallas_call(
        near_kernel,
        out_shape=[
            jax.ShapeDtypeStruct((3, size * rows, feats), bf16) for size in (2, 2, 4)
        ]
        + [jax.ShapeDtypeStruct((2,) + own.shape, bf16)],
        in_specs=[SMEM] + [VMEM] * 7,
        out_specs=[VMEM] * 4,
        compiler_params=PARAMS,
        cost_estimate=cost(0, part_a.size * 14 + own.size * 8),
        name="near",
    )(place[None], part_a, got_a, part_b, got_b, own, back2, back4)


def fast_output(query, hold):
    gate_q = lax.dot_general(
        query, hold[0], (((1,), (1,)), ((), ())), preferred_element_type=f32
    )
    up_q = lax.dot_general(query, hold[1], (((1,), (1,)), ((), ())), preferred_element_type=f32)
    hidden_q = (gate_q * jax.nn.sigmoid(gate_q) * up_q).astype(bf16)
    return jnp.dot(hidden_q, hold[2], preferred_element_type=f32)


def first_kernel(q_ref, near, near_other, out_ref, hold):
    rows = near.shape[1]
    hold[:, :rows] = near[...]
    hold[:, rows:] = near_other[...]
    out_ref[...] = fast_output(q_ref[...], hold)


def first_half(query, near, near_other):
    rows, feats = query.shape
    units = 2 * near.shape[1]
    return pl.pallas_call(
        first_kernel,
        out_shape=jax.ShapeDtypeStruct((rows, feats), f32),
        in_specs=[VMEM] * 3,
        out_specs=VMEM,
        scratch_shapes=[pltpu.VMEM((3, units, feats), bf16)],
        compiler_params=PARAMS,
        cost_estimate=cost(6 * rows * units * feats, 12 * units * feats, units * rows),
        name="first_half",
    )(query, near, near_other)


def far_kernel(got_a, got_b, attended, half_out, far, passed, passed_half):
    del attended, half_out, passed, passed_half
    rows = got_a.shape[1]
    far[:, :rows] = got_a[...]
    far[:, rows:] = got_b[...]


def far_rows(got_a, got_b, attended, half_out):
    shape = (3, 2 * got_a.shape[1], got_a.shape[2])
    return pl.pallas_call(
        far_kernel,
        out_shape=[
            jax.ShapeDtypeStruct(shape, bf16),
            jax.ShapeDtypeStruct(attended.shape, bf16),
            jax.ShapeDtypeStruct(half_out.shape, f32),
        ],
        in_specs=[VMEM] * 2 + [ANY] * 2,
        out_specs=[VMEM, ANY, ANY],
        input_output_aliases={2: 1, 3: 2},
        compiler_params=PARAMS,
        cost_estimate=cost(0, got_a.size * 8),
        name="far",
    )(got_a, got_b, attended, half_out)


def last_kernel(q_ref, half_out, far, far_other, out_ref, hold):
    rows = far.shape[1]
    hold[:, :rows] = far[...]
    hold[:, rows:] = far_other[...]
    out_ref[...] = (half_out[...] + fast_output(q_ref[...], hold)).astype(bf16)


def last_half(query, half_out, far, far_other):
    rows, feats = query.shape
    units = 2 * far.shape[1]
    return pl.pallas_call(
        last_kernel,
        out_shape=jax.ShapeDtypeStruct((rows, feats), bf16),
        in_specs=[VMEM] * 4,
        out_specs=VMEM,
        scratch_shapes=[pltpu.VMEM((3, units, feats), bf16)],
        compiler_params=PARAMS,
        cost_estimate=cost(6 * rows * units * feats, 12 * units * feats, units * rows),
        name="last_half",
    )(query, half_out, far, far_other)


def body(att_q, att_k, att_v, fast_q, fast_k, fast_v, learn_rates, w_gate, w_up, w_down):
    count = lax.axis_size("seq")
    place = lax.axis_index("seq")
    feats, hidden = w_gate.shape
    quart = hidden // 8
    later = [1 << at for at in range(3, count.bit_length() - 1)]
    own_bit = {bit: (place // bit) % 2 for bit in [2, 4] + later}

    other_k, other_v = swapped(fast_k, 1), swapped(fast_v, 1)
    other_r = swapped(learn_rates, 1)
    turned_w = prepared(place, w_gate, w_up, w_down)
    send, keep, own = gradients(
        place, turned_w, fast_k, other_k, fast_v, other_v,
        learn_rates[None, :], other_r[None, :], att_k, att_v,
    )
    back4 = lax.ppermute(own, "seq", [(at, (at + 4) % count) for at in range(count)])
    send, keep = second_sum(place, keep, swapped(send, 2))
    window = window_step(place, own, back4, send)
    back2 = swapped(window, 2)
    grads, send = third_sum(keep, swapped(send, 4), window)
    rest = quart
    start = own_bit[2] * 2 * quart + own_bit[4] * quart
    for bit in later[:-1]:
        rest //= 2
        grads = grads.reshape(3, 2, rest, feats)
        send = lax.dynamic_index_in_dim(grads, 1 - own_bit[bit], 1, keepdims=False)
        grads = lax.dynamic_index_in_dim(grads, own_bit[bit], 1, keepdims=False)
        grads = grads + swapped(send.astype(bf16), bit).astype(f32)
        send = grads.astype(bf16)
        start += own_bit[bit] * rest
    got = swapped(send, later[-1])
    old = lax.dynamic_slice_in_dim(turned_w, start, rest, 1)
    part_a, part_b = renormed(old, grads, got)

    for bit in reversed(later[:-1]):
        part_a = jnp.concatenate([part_a, swapped(part_a, bit)], axis=1)
        part_b = jnp.concatenate([part_b, swapped(part_b, bit)], axis=1)
    near_a, near_b, near, pair = near_rows(
        place, part_a, swapped(part_a, 4), part_b, swapped(part_b, 2), own, back2, back4
    )
    got_a, got_b = swapped(near_a, 2), swapped(near_b, 4)
    near_other = swapped(near, 1)
    pair = swapped(pair, 1)
    attended = attention(place, att_q, own, back2, back4, pair)
    half_out = first_half(fast_q, near, near_other)
    far, attended, half_out = far_rows(got_a, got_b, attended, half_out)
    fast_out = last_half(fast_q, half_out, far, swapped(far, 1))
    return (attended, fast_out)


def solution(mesh):
    tokens = P("seq", "head")
    weights = P(None, "head")
    return jax.shard_map(
        body,
        mesh=mesh,
        in_specs=(tokens,) * 6 + (P("seq"),) + (weights,) * 3,
        out_specs=(tokens, tokens),
        check_vma=False,
    )
```

profile of v0, /device:TPU:0, one launch (start us, length us, event | category | flops | bytes accessed | tf_op | source)
XLA Modules:
  0.0 73.7 jit_solution(15161718706154170541)
XLA Ops:
  0.6 0.5 collective-permute-start
  1.2 0.4 collective-permute-start.2
  1.7 3.0 %prepare.1.turned_ref = bf16[3,320,640]{2,1,0:T(8,128)(2,1)} custom-call(s32[1]{0:T(128)} %bitcast.place_ref, bf16[640,640]{1,0:T(8,128)(2,1)} %gate_ref.1, bf16[640,640]{1,0:T(8,128)(2,1)} %up_ref.1, bf16[640,640]{1,0:T(8,128)(2,1)} %down_ref.1), custom_call_target="tpu_custom_call" | custom-call | bytes 3686400 | tf_op jit(solution)/shard_map/prepare/pallas_call | solution.py:133
  4.8 1.3 %copy-done = bf16[3,320,640]{2,1,0:T(8,128)(2,1)S(1)} copy-done((bf16[3,320,640]{2,1,0:T(8,128)(2,1)S(1)}, bf16[3,320,640]{2,1,0:T(8,128)(2,1)}, u32[]{:S(2)}) %copy-start) | copy-done | bytes 1228824
  6.1 2.4 %gradients.1 = (bf16[3,2,80,640]{3,2,1,0:T(8,128)(2,1)S(1)}, f32[3,2,80,640]{3,2,1,0:T(8,128)S(1)}, bf16[2,256,640]{2,1,0:T(8,128)(2,1)S(1)}) custom-call(s32[1]{0:T(128)} %bitcast.place_ref, bf16[3,320,640]{2,1,0:T(8,128)(2,1)S(1)} %copy-done, bf16[256,640]{1,0:T(8,128)(2,1)S(1)} %copy-done.3, bf16[256,640]{1,0:T(8,128)(2,1)S(1)} %collective-permute-done.k1_ref, ...), custom_call_target="tpu_custom_call" | custom-call | flops 1258291200 | bytes 4096000 | tf_op jit(solution)/shard_map/gradients/pallas_call | solution.py:196
  8.5 2.6 %collective-permute-start.3 = (bf16[3,2,80,640]{3,2,1,0:T(8,128)(2,1)S(1)}, bf16[3,2,80,640]{3,2,1,0:T(8,128)(2,1)S(1)}, u32[]{:S(2)}, u32[]{:S(2)}) collective-permute-start(bf16[3,2,80,640]{3,2,1,0:T(8,128)(2,1)S(1)} %get-tuple-element.19), channel_id=1, source_target_pairs={{0,4},{2,6},{4,0},{6,2},{8,12},{10,14},{12,8},{14,10},{16,20},{18,... | collective-permute-start | bytes 1843208 | tf_op jit(solution)/shard_map/ppermute | solution.py:26
  11.2 1.6 %collective-permute-start.5 = (bf16[2,256,640]{2,1,0:T(8,128)(2,1)S(1)}, bf16[2,256,640]{2,1,0:T(8,128)(2,1)S(1)}, u32[]{:S(2)}, u32[]{:S(2)}) collective-permute-start(bf16[2,256,640]{2,1,0:T(8,128)(2,1)S(1)} %get-tuple-element.22.own_ref), channel_id=1, source_target_pairs={{0,8},{2,10},{4,12},{6,14},{8,16},{10,18},{12,20},{14,22},{16,24},... | collective-permute-start | bytes 1966088 | tf_op jit(solution)/shard_map/ppermute | solution.py:440
  12.7 12.9 %collective-permute-done.3.got = bf16[3,2,80,640]{3,2,1,0:T(8,128)(2,1)S(1)} collective-permute-done((bf16[3,2,80,640]{3,2,1,0:T(8,128)(2,1)S(1)}, bf16[3,2,80,640]{3,2,1,0:T(8,128)(2,1)S(1)}, u32[]{:S(2)}, u32[]{:S(2)}) %collective-permute-start.3) | collective-permute-done | bytes 614432 | tf_op jit(solution)/shard_map/ppermute | solution.py:26
  25.6 0.1 second.1
  25.8 1.9 %collective-permute-start.4 = (bf16[3,80,640]{2,1,0:T(8,128)(2,1)S(1)}, bf16[3,80,640]{2,1,0:T(8,128)(2,1)S(1)}, u32[]{:S(2)}, u32[]{:S(2)}) collective-permute-start(bf16[3,80,640]{2,1,0:T(8,128)(2,1)S(1)} %get-tuple-element.21.tied), channel_id=1, source_target_pairs={{0,8},{2,10},{4,12},{6,14},{8,0},{10,2},{12,4},{14,6},{16,24},{18,... | collective-permute-start | bytes 921608 | tf_op jit(solution)/shard_map/ppermute | solution.py:26
  27.6 2.3 %collective-permute-done.5.back_ref.back4_ref = bf16[2,256,640]{2,1,0:T(8,128)(2,1)S(1)} collective-permute-done((bf16[2,256,640]{2,1,0:T(8,128)(2,1)S(1)}, bf16[2,256,640]{2,1,0:T(8,128)(2,1)S(1)}, u32[]{:S(2)}, u32[]{:S(2)}) %collective-permute-start.5) | collective-permute-done | bytes 655392 | tf_op jit(solution)/shard_map/ppermute | solution.py:440
  30.0 0.5 collective-permute-start.9
  30.5 5.9 %collective-permute-done.4.got = bf16[3,80,640]{2,1,0:T(8,128)(2,1)S(1)} collective-permute-done((bf16[3,80,640]{2,1,0:T(8,128)(2,1)S(1)}, bf16[3,80,640]{2,1,0:T(8,128)(2,1)S(1)}, u32[]{:S(2)}, u32[]{:S(2)}) %collective-permute-start.4) | collective-permute-done | bytes 307232 | tf_op jit(solution)/shard_map/ppermute | solution.py:26
  36.4 0.8 %third.1 = (f32[3,80,640]{2,1,0:T(8,128)S(1)}, bf16[3,80,640]{2,1,0:T(8,128)(2,1)}) custom-call(f32[3,80,640]{2,1,0:T(8,128)S(1)} %get-tuple-element.20.keep, bf16[3,80,640]{2,1,0:T(8,128)(2,1)S(1)} %collective-permute-done.4.got, bf16[2,256,640]{2,1,0:T(8,128)(2,1)S(1)} %window.1.tied), custom_call_target="tpu_custom_call" | custom-call | flops 307200 | bytes 1228800 | tf_op jit(solution)/shard_map/third/pallas_call | solution.py:241
  37.2 1.1 %collective-permute-start.6 = (bf16[3,80,640]{2,1,0:T(8,128)(2,1)}, bf16[3,80,640]{2,1,0:T(8,128)(2,1)S(1)}, u32[]{:S(2)}, u32[]{:S(2)}) collective-permute-start(bf16[3,80,640]{2,1,0:T(8,128)(2,1)} %get-tuple-element.24), channel_id=1, source_target_pairs={{0,16},{2,18},{4,20},{6,22},{8,24},{10,26},{12,28},{14,30},{16,0},... | collective-permute-start | bytes 921608 | tf_op jit(solution)/shard_map/ppermute | solution.py:26
  38.3 1.0 %constant_dynamic-slice_fusion.old_ref = bf16[3,80,640]{2,1,0:T(8,128)(2,1)S(1)} fusion(bf16[3,320,640]{2,1,0:T(8,128)(2,1)} %prepare.1.turned_ref, s32[]{:T(128)S(6)} %select_n.25), kind=kLoop, calls=%fused_computation | loop fusion | bytes 614404 | tf_op jit(solution)/shard_map/dynamic_slice | solution.py:456
  39.3 13.8 %collective-permute-done.6.got = bf16[3,80,640]{2,1,0:T(8,128)(2,1)S(1)} collective-permute-done((bf16[3,80,640]{2,1,0:T(8,128)(2,1)}, bf16[3,80,640]{2,1,0:T(8,128)(2,1)S(1)}, u32[]{:S(2)}, u32[]{:S(2)}) %collective-permute-start.6) | collective-permute-done | bytes 307232 | tf_op jit(solution)/shard_map/ppermute | solution.py:26
  53.1 0.3 renorm.1
  53.5 0.9 %collective-permute-start.8 = (bf16[3,40,640]{2,1,0:T(8,128)(2,1)S(1)}, bf16[3,40,640]{2,1,0:T(8,128)(2,1)S(1)}, u32[]{:S(2)}, u32[]{:S(2)}) collective-permute-start(bf16[3,40,640]{2,1,0:T(8,128)(2,1)S(1)} %get-tuple-element.26.part_b), channel_id=1, source_target_pairs={{0,4},{2,6},{4,0},{6,2},{8,12},{10,14},{12,8},{14,10},{16,20},{18,... | collective-permute-start | bytes 460808 | tf_op jit(solution)/shard_map/ppermute | solution.py:26
  54.3 5.0 %collective-permute-done.7.got_a = bf16[3,40,640]{2,1,0:T(8,128)(2,1)S(1)} collective-permute-done((bf16[3,40,640]{2,1,0:T(8,128)(2,1)S(1)}, bf16[3,40,640]{2,1,0:T(8,128)(2,1)S(1)}, u32[]{:S(2)}, u32[]{:S(2)}) %collective-permute-start.7) | collective-permute-done | bytes 153632 | tf_op jit(solution)/shard_map/ppermute | solution.py:26
  59.3 0.1 collective-permute-done.8.got_b
  59.4 0.2 near.1
  59.7 0.5 collective-permute-start.13
  60.2 0.8 %collective-permute-start.10 = (bf16[3,80,640]{2,1,0:T(8,128)(2,1)S(1)}, bf16[3,80,640]{2,1,0:T(8,128)(2,1)S(1)}, u32[]{:S(2)}, u32[]{:S(2)}) collective-permute-start(bf16[3,80,640]{2,1,0:T(8,128)(2,1)S(1)} %get-tuple-element.27), channel_id=1, source_target_pairs={{0,4},{2,6},{4,0},{6,2},{8,12},{10,14},{12,8},{14,10},{16,20},{18,... | collective-permute-start | bytes 921608 | tf_op jit(solution)/shard_map/ppermute | solution.py:26
  61.0 1.7 %collective-permute-start.11 = (bf16[3,80,640]{2,1,0:T(8,128)(2,1)S(1)}, bf16[3,80,640]{2,1,0:T(8,128)(2,1)S(1)}, u32[]{:S(2)}, u32[]{:S(2)}) collective-permute-start(bf16[3,80,640]{2,1,0:T(8,128)(2,1)S(1)} %get-tuple-element.28), channel_id=1, source_target_pairs={{0,8},{2,10},{4,12},{6,14},{8,0},{10,2},{12,4},{14,6},{16,24},{18,... | collective-permute-start | bytes 921608 | tf_op jit(solution)/shard_map/ppermute | solution.py:26
  62.7 1.0 %collective-permute-done.13.near_other = bf16[3,160,640]{2,1,0:T(8,128)(2,1)S(1)} collective-permute-done((bf16[3,160,640]{2,1,0:T(8,128)(2,1)S(1)}, bf16[3,160,640]{2,1,0:T(8,128)(2,1)S(1)}, u32[]{:S(2)}, u32[]{:S(2)}) %collective-permute-start.13) | collective-permute-done | bytes 614432 | tf_op jit(solution)/shard_map/ppermute | solution.py:26
  63.6 0.8 %first_half.1.half_out = f32[256,640]{1,0:T(8,128)S(1)} custom-call(bf16[256,640]{1,0:T(8,128)(2,1)S(1)} %copy-done.1, bf16[3,160,640]{2,1,0:T(8,128)(2,1)S(1)} %get-tuple-element.30.near, bf16[3,160,640]{2,1,0:T(8,128)(2,1)S(1)} %collective-permute-done.13.near_other), custom_call_target="tpu_custom_call" | custom-call | flops 314572800 | bytes 2457600 | tf_op jit(solution)/shard_map/first_half/pallas_call | solution.py:366
  64.5 4.7 %attention.1.attended = bf16[256,640]{1,0:T(8,128)(2,1)} custom-call(s32[1]{0:T(128)} %bitcast.place_ref, bf16[256,640]{1,0:T(8,128)(2,1)S(1)} %copy-done.2, bf16[2,256,640]{2,1,0:T(8,128)(2,1)S(1)} %get-tuple-element.22.own_ref, bf16[2,256,640]{2,1,0:T(8,128)(2,1)S(1)} %collective-permute-done.9.back2_ref, ...), custom_call_target="tpu_custom_call" | custom-call | flops 838860800 | bytes 3932160 | tf_op jit(solution)/shard_map/attention/pallas_call | solution.py:88
  69.2 0.3 collective-permute-done.10.got_a
  69.5 0.5 collective-permute-done.11.got_b
  70.1 2.0 %collective-permute-done.14.far_other = bf16[3,160,640]{2,1,0:T(8,128)(2,1)S(1)} collective-permute-done((bf16[3,160,640]{2,1,0:T(8,128)(2,1)S(1)}, bf16[3,160,640]{2,1,0:T(8,128)(2,1)S(1)}, u32[]{:S(2)}, u32[]{:S(2)}) %collective-permute-start.14) | collective-permute-done | bytes 614432 | tf_op jit(solution)/shard_map/ppermute | solution.py:26
  72.2 1.6 %last_half.1 = bf16[256,640]{1,0:T(8,128)(2,1)} custom-call(bf16[256,640]{1,0:T(8,128)(2,1)S(1)} %copy-done.1, f32[256,640]{1,0:T(8,128)S(1)} %get-tuple-element.32.half_out, bf16[3,160,640]{2,1,0:T(8,128)(2,1)S(1)} %get-tuple-element.33.far, bf16[3,160,640]{2,1,0:T(8,128)(2,1)S(1)} %collective-permute-done.14.far_other), custom_call_target="tpu_custom_call" | custom-call | flops 314572800 | bytes 2457600 | tf_op jit(solution)/shard_map/last_half/pallas_call | solution.py:413
  (26 shorter events, 0.4 us)
Async XLA Ops:
  0.6 4.1 %collective-permute-start = (bf16[256,640]{1,0:T(8,128)(2,1)}, bf16[256,640]{1,0:T(8,128)(2,1)S(1)}, u32[]{:S(2)}, u32[]{:S(2)}) collective-permute-start(bf16[256,640]{1,0:T(8,128)(2,1)} %k0_ref.1), channel_id=1, source_target_pairs={{0,2},{2,0},{4,6},{6,4},{8,10},{10,8},{12,14},{14,12},{16,18},{18,... | collective-permute-start | bytes 983048 | tf_op jit(solution)/shard_map/ppermute | solution.py:26
  1.2 3.6 %collective-permute-start.1 = (bf16[256,640]{1,0:T(8,128)(2,1)}, bf16[256,640]{1,0:T(8,128)(2,1)S(1)}, u32[]{:S(2)}, u32[]{:S(2)}) collective-permute-start(bf16[256,640]{1,0:T(8,128)(2,1)} %v0_ref.1), channel_id=1, source_target_pairs={{0,2},{2,0},{4,6},{6,4},{8,10},{10,8},{12,14},{14,12},{16,18},{18,... | collective-permute-start | bytes 983048 | tf_op jit(solution)/shard_map/ppermute | solution.py:26
  1.2 3.5 %collective-permute-start.2 = (f32[256]{0:T(256)}, f32[256]{0:T(256)S(1)}, u32[]{:S(2)}, u32[]{:S(2)}) collective-permute-start(f32[256]{0:T(256)} %param.16), channel_id=1, source_target_pairs={{0,2},{2,0},{4,6},{6,4},{8,10},{10,8},{12,14},{14,12},{16,18},{18,... | collective-permute-start | bytes 3080 | tf_op jit(solution)/shard_map/ppermute | solution.py:26
  1.7 3.1 %copy-start.3 = (bf16[256,640]{1,0:T(8,128)(2,1)S(1)}, bf16[256,640]{1,0:T(8,128)(2,1)}, u32[]{:S(2)}) copy-start(bf16[256,640]{1,0:T(8,128)(2,1)} %k0_ref.1) | copy-start | bytes 983044
  1.7 3.1 %copy-start.4 = (bf16[256,640]{1,0:T(8,128)(2,1)S(1)}, bf16[256,640]{1,0:T(8,128)(2,1)}, u32[]{:S(2)}) copy-start(bf16[256,640]{1,0:T(8,128)(2,1)} %v0_ref.1) | copy-start | bytes 983044
  1.7 3.1 %copy-start.5 = (bf16[256,640]{1,0:T(8,128)(2,1)S(1)}, bf16[256,640]{1,0:T(8,128)(2,1)}, u32[]{:S(2)}) copy-start(bf16[256,640]{1,0:T(8,128)(2,1)} %key_ref.1) | copy-start | bytes 983044
  1.7 3.1 %copy-start.6 = (bf16[256,640]{1,0:T(8,128)(2,1)S(1)}, bf16[256,640]{1,0:T(8,128)(2,1)}, u32[]{:S(2)}) copy-start(bf16[256,640]{1,0:T(8,128)(2,1)} %val_ref.1) | copy-start | bytes 983044
  1.7 3.1 %copy-start.7 = (f32[256]{0:T(256)S(1)}, f32[256]{0:T(256)}, u32[]{:S(2)}) copy-start(f32[256]{0:T(256)} %param.16) | copy-start | bytes 3076
  4.8 1.3 %copy-start = (bf16[3,320,640]{2,1,0:T(8,128)(2,1)S(1)}, bf16[3,320,640]{2,1,0:T(8,128)(2,1)}, u32[]{:S(2)}) copy-start(bf16[3,320,640]{2,1,0:T(8,128)(2,1)} %prepare.1.turned_ref) | copy-start | bytes 3686404
  8.5 17.1 %collective-permute-start.3 = (bf16[3,2,80,640]{3,2,1,0:T(8,128)(2,1)S(1)}, bf16[3,2,80,640]{3,2,1,0:T(8,128)(2,1)S(1)}, u32[]{:S(2)}, u32[]{:S(2)}) collective-permute-start(bf16[3,2,80,640]{3,2,1,0:T(8,128)(2,1)S(1)} %get-tuple-element.19), channel_id=1, source_target_pairs={{0,4},{2,6},{4,0},{6,2},{8,12},{10,14},{12,8},{14,10},{16,20},{18,... | collective-permute-start | bytes 1843208 | tf_op jit(solution)/shard_map/ppermute | solution.py:26
  11.2 18.8 %collective-permute-start.5 = (bf16[2,256,640]{2,1,0:T(8,128)(2,1)S(1)}, bf16[2,256,640]{2,1,0:T(8,128)(2,1)S(1)}, u32[]{:S(2)}, u32[]{:S(2)}) collective-permute-start(bf16[2,256,640]{2,1,0:T(8,128)(2,1)S(1)} %get-tuple-element.22.own_ref), channel_id=1, source_target_pairs={{0,8},{2,10},{4,12},{6,14},{8,16},{10,18},{12,20},{14,22},{16,24},... | collective-permute-start | bytes 1966088 | tf_op jit(solution)/shard_map/ppermute | solution.py:440
  25.8 10.6 %collective-permute-start.4 = (bf16[3,80,640]{2,1,0:T(8,128)(2,1)S(1)}, bf16[3,80,640]{2,1,0:T(8,128)(2,1)S(1)}, u32[]{:S(2)}, u32[]{:S(2)}) collective-permute-start(bf16[3,80,640]{2,1,0:T(8,128)(2,1)S(1)} %get-tuple-element.21.tied), channel_id=1, source_target_pairs={{0,8},{2,10},{4,12},{6,14},{8,0},{10,2},{12,4},{14,6},{16,24},{18,... | collective-permute-start | bytes 921608 | tf_op jit(solution)/shard_map/ppermute | solution.py:26
  30.0 24.3 %collective-permute-start.9 = (bf16[2,256,640]{2,1,0:T(8,128)(2,1)S(1)}, bf16[2,256,640]{2,1,0:T(8,128)(2,1)S(1)}, u32[]{:S(2)}, u32[]{:S(2)}) collective-permute-start(bf16[2,256,640]{2,1,0:T(8,128)(2,1)S(1)} %window.1.tied), channel_id=1, source_target_pairs={{0,4},{2,6},{4,0},{6,2},{8,12},{10,14},{12,8},{14,10},{16,20},{18,... | collective-permute-start | bytes 1966088 | tf_op jit(solution)/shard_map/ppermute | solution.py:26
  37.2 15.9 %collective-permute-start.6 = (bf16[3,80,640]{2,1,0:T(8,128)(2,1)}, bf16[3,80,640]{2,1,0:T(8,128)(2,1)S(1)}, u32[]{:S(2)}, u32[]{:S(2)}) collective-permute-start(bf16[3,80,640]{2,1,0:T(8,128)(2,1)} %get-tuple-element.24), channel_id=1, source_target_pairs={{0,16},{2,18},{4,20},{6,22},{8,24},{10,26},{12,28},{14,30},{16,0},... | collective-permute-start | bytes 921608 | tf_op jit(solution)/shard_map/ppermute | solution.py:26
  53.4 6.0 %collective-permute-start.7 = (bf16[3,40,640]{2,1,0:T(8,128)(2,1)S(1)}, bf16[3,40,640]{2,1,0:T(8,128)(2,1)S(1)}, u32[]{:S(2)}, u32[]{:S(2)}) collective-permute-start(bf16[3,40,640]{2,1,0:T(8,128)(2,1)S(1)} %get-tuple-element.25.part_a), channel_id=1, source_target_pairs={{0,8},{2,10},{4,12},{6,14},{8,0},{10,2},{12,4},{14,6},{16,24},{18,... | collective-permute-start | bytes 460808 | tf_op jit(solution)/shard_map/ppermute | solution.py:26
  53.5 10.2 %copy-start.1 = (bf16[256,640]{1,0:T(8,128)(2,1)S(1)}, bf16[256,640]{1,0:T(8,128)(2,1)}, u32[]{:S(2)}) copy-start(bf16[256,640]{1,0:T(8,128)(2,1)} %q_ref.5) | copy-start | bytes 983044
  53.5 6.0 %collective-permute-start.8 = (bf16[3,40,640]{2,1,0:T(8,128)(2,1)S(1)}, bf16[3,40,640]{2,1,0:T(8,128)(2,1)S(1)}, u32[]{:S(2)}, u32[]{:S(2)}) collective-permute-start(bf16[3,40,640]{2,1,0:T(8,128)(2,1)S(1)} %get-tuple-element.26.part_b), channel_id=1, source_target_pairs={{0,4},{2,6},{4,0},{6,2},{8,12},{10,14},{12,8},{14,10},{16,20},{18,... | collective-permute-start | bytes 460808 | tf_op jit(solution)/shard_map/ppermute | solution.py:26
  59.6 4.8 %copy-start.2 = (bf16[256,640]{1,0:T(8,128)(2,1)S(1)}, bf16[256,640]{1,0:T(8,128)(2,1)}, u32[]{:S(2)}) copy-start(bf16[256,640]{1,0:T(8,128)(2,1)} %q_ref.3) | copy-start | bytes 983044
  59.7 4.8 %collective-permute-start.12 = (bf16[2,2,256,640]{3,2,1,0:T(8,128)(2,1)S(1)}, bf16[2,2,256,640]{3,2,1,0:T(8,128)(2,1)S(1)}, u32[]{:S(2)}, u32[]{:S(2)}) collective-permute-start(bf16[2,2,256,640]{3,2,1,0:T(8,128)(2,1)S(1)} %get-tuple-element.29), channel_id=1, source_target_pairs={{0,2},{2,0},{4,6},{6,4},{8,10},{10,8},{12,14},{14,12},{16,18},{18,... | collective-permute-start | bytes 3932168 | tf_op jit(solution)/shard_map/ppermute | solution.py:26
  59.7 3.9 %collective-permute-start.13 = (bf16[3,160,640]{2,1,0:T(8,128)(2,1)S(1)}, bf16[3,160,640]{2,1,0:T(8,128)(2,1)S(1)}, u32[]{:S(2)}, u32[]{:S(2)}) collective-permute-start(bf16[3,160,640]{2,1,0:T(8,128)(2,1)S(1)} %get-tuple-element.30.near), channel_id=1, source_target_pairs={{0,2},{2,0},{4,6},{6,4},{8,10},{10,8},{12,14},{14,12},{16,18},{18,... | collective-permute-start | bytes 1843208 | tf_op jit(solution)/shard_map/ppermute | solution.py:26
  60.2 9.3 %collective-permute-start.10 = (bf16[3,80,640]{2,1,0:T(8,128)(2,1)S(1)}, bf16[3,80,640]{2,1,0:T(8,128)(2,1)S(1)}, u32[]{:S(2)}, u32[]{:S(2)}) collective-permute-start(bf16[3,80,640]{2,1,0:T(8,128)(2,1)S(1)} %get-tuple-element.27), channel_id=1, source_target_pairs={{0,4},{2,6},{4,0},{6,2},{8,12},{10,14},{12,8},{14,10},{16,20},{18,... | collective-permute-start | bytes 921608 | tf_op jit(solution)/shard_map/ppermute | solution.py:26
  61.0 9.0 %collective-permute-start.11 = (bf16[3,80,640]{2,1,0:T(8,128)(2,1)S(1)}, bf16[3,80,640]{2,1,0:T(8,128)(2,1)S(1)}, u32[]{:S(2)}, u32[]{:S(2)}) collective-permute-start(bf16[3,80,640]{2,1,0:T(8,128)(2,1)S(1)} %get-tuple-element.28), channel_id=1, source_target_pairs={{0,8},{2,10},{4,12},{6,14},{8,0},{10,2},{12,4},{14,6},{16,24},{18,... | collective-permute-start | bytes 921608 | tf_op jit(solution)/shard_map/ppermute | solution.py:26
  70.0 2.1 %collective-permute-start.14 = (bf16[3,160,640]{2,1,0:T(8,128)(2,1)S(1)}, bf16[3,160,640]{2,1,0:T(8,128)(2,1)S(1)}, u32[]{:S(2)}, u32[]{:S(2)}) collective-permute-start(bf16[3,160,640]{2,1,0:T(8,128)(2,1)S(1)} %get-tuple-element.33.far), channel_id=1, source_target_pairs={{0,2},{2,0},{4,6},{6,4},{8,10},{10,8},{12,14},{14,12},{16,18},{18,... | collective-permute-start | bytes 1843208 | tf_op jit(solution)/shard_map/ppermute | solution.py:26
where the time goes:
time: 73.9 us; the launch traced here: 73.7 us
  waiting for transfers between devices  43.8 us (59%)
  Pallas kernels  14.1 us (19%)
  starting transfers between devices  12.7 us (17%)
  local copies, waits for them, and re-layouts  2.3 us (3%)
  between operations  0.83 us (1%)
    ppermute x14, waiting for transfers between devices, swapped(): return lax.ppermute(value, 'seq', [(at, at ^ bit) for at in range(count)])  41.5 us
    ppermute x14, starting transfers between devices, swapped(): return lax.ppermute(value, 'seq', [(at, at ^ bit) for at in range(count)])  11.2 us
    pallas_call x1, Pallas kernels, attention(): pl.pallas_call(attention_kernel, out_shape=jax.ShapeDtypeStruct((rows, wi...  4.72 us
    pallas_call x1, Pallas kernels, prepared(): pl.pallas_call(prepare_kernel, out_shape=jax.ShapeDtypeStruct((3, half, f...  3.03 us
    pallas_call x1, Pallas kernels, gradients(): pl.pallas_call(grad_kernel, out_shape=[jax.ShapeDtypeStruct(shape, bf16),...  2.43 us
    ppermute x1, waiting for transfers between devices, body(): lax.ppermute(own, 'seq', [(at, (at + 4) % count) for at in range(count)])  2.3 us
    ppermute x1, starting transfers between devices, body(): lax.ppermute(own, 'seq', [(at, (at + 4) % count) for at in range(count)])  1.58 us
    pallas_call x1, Pallas kernels, last_half(): pl.pallas_call(last_kernel, out_shape=jax.ShapeDtypeStruct((rows, feats),...  1.56 us
  transfers between devices with their start and end apart: 15, of which 10 were waited for; matrix products, arithmetic and copies ran while one was open for 1% of the time, Pallas kernels for 13%

commit v1 on v0

v1 whole, which is shorter than its diff:
```python
import functools
import math

import jax
import jax.numpy as jnp
from jax import lax
from jax.experimental import pallas as pl
from jax.experimental.pallas import tpu as pltpu
from jax.sharding import PartitionSpec as P

WINDOW = 1024
HEAD_DIM = 128
norm_eps = 1e-06
f32 = jnp.float32
bf16 = jnp.bfloat16

SMEM = pl.BlockSpec(memory_space=pltpu.SMEM)
VMEM = pl.BlockSpec(memory_space=pltpu.VMEM)
HBM = pl.BlockSpec(memory_space=pltpu.HBM)
ANY = pl.BlockSpec(memory_space=pl.ANY)
PARAMS = pltpu.CompilerParams(vmem_limit_bytes=16 << 20)


def swapped(value, bit):
    count = lax.axis_size("seq")
    return lax.ppermute(value, "seq", [(at, at ^ bit) for at in range(count)])


def kernel_call(kernel, operands, tied=(), in_specs=None, name=None, **rest):
    given = len(operands)

    def run(*refs):
        kernel(*refs[:given], *refs[given + len(tied) :])

    return pl.pallas_call(
        run, in_specs=list(in_specs) + [ANY] * len(tied), name=name, **rest
    )(*operands, *tied)


def cost(flops, moved_bytes, exps=0):
    return pl.CostEstimate(flops=flops, bytes_accessed=moved_bytes, transcendentals=exps)


def attention_kernel(
    place_ref, q_ref, own_k, own_v, back2_k, back2_v, back4_k, back4_v, pair_ref, out_ref
):
    keys = [own_k, back4_k, pair_ref.at[0, 0], back2_k, pair_ref.at[1, 0]]
    vals = [own_v, back4_v, pair_ref.at[0, 1], back2_v, pair_ref.at[1, 1]]
    rows, width = q_ref.shape
    place = place_ref[0]
    factor = HEAD_DIM ** (-0.5) * math.log2(math.e)
    q_at = lax.broadcasted_iota(jnp.int32, (rows, rows), 0)
    k_at = lax.broadcasted_iota(jnp.int32, (rows, rows), 1)
    inside = k_at <= q_at

    def attend(cols, masked):
        query = q_ref[:, cols]

        def score(at):
            return lax.dot_general(
                query, keys[at][:, cols], (((1,), (1,)), ((), ())), preferred_element_type=f32
            )

        def seen(part, back):
            return jnp.where(place >= back, part, -1e30) if masked else part

        parts = [jnp.where(inside, score(0), seen(score(1), 4))]
        parts += [seen(score(at), at - 1) for at in range(2, 5)]
        row_max = functools.reduce(
            jnp.maximum, [jnp.max(part, axis=1, keepdims=True) for part in parts]
        )
        shift = row_max * factor
        parts = [jnp.exp2(part * factor - shift) for part in parts]
        total = functools.reduce(jnp.add, [jnp.sum(e, axis=1, keepdims=True) for e in parts])
        scale = 1.0 / total
        parts = [(part * scale).astype(bf16) for part in parts]
        zero = jnp.zeros_like(parts[0])
        parts = [jnp.where(inside, parts[0], zero), jnp.where(inside, zero, parts[0])] + parts[1:]
        result = jnp.zeros((rows, HEAD_DIM), f32)
        for part, val in zip(parts, vals):
            result += jnp.dot(part, val[:, cols], preferred_element_type=f32)
        out_ref[:, cols] = result.astype(bf16)

    def every(masked):
        for head in range(width // HEAD_DIM):
            attend(slice(head * HEAD_DIM, (head + 1) * HEAD_DIM), masked)

    pl.when(place >= 4)(lambda: every(False))
    pl.when(place < 4)(lambda: every(True))


def attention(place, query, blocks, pair):
    rows, width = query.shape
    return pl.pallas_call(
        attention_kernel,
        out_shape=jax.ShapeDtypeStruct((rows, width), bf16),
        in_specs=[SMEM] + [VMEM] * 8,
        out_specs=VMEM,
        compiler_params=PARAMS,
        cost_estimate=cost(20 * rows * rows * width, 24 * rows * width, 5 * rows * rows * 5),
        name="attention",
    )(place[None], query, *blocks, pair)


def prepare_kernel(place_ref, gate_ref, up_ref, down_ref, out_ref, hold):
    hidden = gate_ref.shape[1]
    half = hidden // 2
    window = hold.shape[0]
    core = place_ref[0] % 2
    low = pl.multiple_of(core * (hidden - window), 128)
    off = pl.multiple_of(core * (half - hidden + window), 64)
    for at, ref in enumerate((gate_ref, up_ref, down_ref)):
        hold[...] = ref[:, pl.ds(low, window)].T
        out_ref[at] = hold[pl.ds(off, half), :]


def prepared(place, w_gate, w_up, w_down):
    feats, hidden = w_gate.shape
    half = hidden // 2
    window = -(-half // 128) * 128
    return pl.pallas_call(
        prepare_kernel,
        out_shape=jax.ShapeDtypeStruct((3, half, feats), bf16),
        in_specs=[SMEM] + [VMEM] * 3,
        out_specs=VMEM,
        scratch_shapes=[pltpu.VMEM((window, feats), bf16)],
        compiler_params=PARAMS,
        cost_estimate=cost(0, 9 * feats * hidden),
        name="prepare",
    )(place[None], w_gate, w_up, w_down)


def grad_kernel(
    place_ref, turned_ref, k0_ref, k1_ref, v0_ref, v1_ref, r0_ref, r1_ref, key_ref, val_ref,
    send_p, send_q, keep_p, keep_q, own_k, own_v, hold,
):
    own_k[...] = key_ref[...]
    own_v[...] = val_ref[...]

    def project(at, rows):
        return lax.dot_general(
            turned_ref[at], rows, (((1,), (1,)), ((), ())), preferred_element_type=f32
        )

    terms = []
    for keys, vals, rate_ref in ((k0_ref, v0_ref, r0_ref), (k1_ref, v1_ref, r1_ref)):
        rate = rate_ref[...]
        pre_gate = project(0, keys[...])
        pre_up = project(1, keys[...])
        back = rate * project(2, vals[...])
        sigmoid_v = jax.nn.sigmoid(pre_gate)
        silu = pre_gate * sigmoid_v
        slope = sigmoid_v * (1.0 + pre_gate * (1.0 - sigmoid_v))
        terms.append(
            (
                (back * pre_up * slope).astype(bf16),
                (back * silu).astype(bf16),
                (rate * silu * pre_up).astype(bf16),
            )
        )
    sources = ((k0_ref, k1_ref), (k0_ref, k1_ref), (v0_ref, v1_ref))
    for at in range(3):
        hold[at] = jnp.dot(
            terms[0][at], sources[at][0][...], preferred_element_type=f32
        ) + jnp.dot(terms[1][at], sources[at][1][...], preferred_element_type=f32)
    quart = send_p.shape[2]
    row = (place_ref[0] // 2) % 2
    for at in range(3):
        send, keep = (send_p.at[at], keep_p.at[at]) if at < 2 else (send_q.at[0], keep_q.at[0])
        for other in range(2):
            there = pl.multiple_of((2 * (1 - row) + other) * quart, 8)
            here = pl.multiple_of((2 * row + other) * quart, 8)
            send[other] = hold[at, pl.ds(there, quart), :].astype(bf16)
            keep[other] = hold[at, pl.ds(here, quart), :]


def gradients(place, turned_w, k0, k1, v0, v1, r0, r1, att_k, att_v):
    _, half, feats = turned_w.shape
    rows = k0.shape[0]
    return pl.pallas_call(
        grad_kernel,
        out_shape=[
            jax.ShapeDtypeStruct((count, 2, half // 4, feats), kind)
            for kind in (bf16, f32)
            for count in (2, 1)
        ]
        + [jax.ShapeDtypeStruct(att_k.shape, bf16)] * 2,
        in_specs=[SMEM] + [VMEM] * 9,
        out_specs=[VMEM] * 6,
        scratch_shapes=[pltpu.VMEM((3, half, feats), f32)],
        compiler_params=PARAMS,
        cost_estimate=cost(24 * rows * half * feats, 20 * half * feats, 2 * half * rows),
        name="gradients",
    )(place[None], turned_w, k0, k1, v0, v1, r0, r1, att_k, att_v)


def stage(kernel, operands, outs, name, *tied):
    return kernel_call(
        kernel,
        (operands[0][None], *operands[1:]),
        tied,
        out_shape=[jax.ShapeDtypeStruct(shape, kind) for shape, kind in outs],
        in_specs=[SMEM] + [VMEM] * (len(operands) - 1),
        out_specs=[VMEM] * len(outs),
        compiler_params=PARAMS,
        cost_estimate=cost(0, 0),
        name=name,
    )


def halve(place_ref, keep, got, send, kept):
    row = (place_ref[0] // 4) % 2
    for at in range(keep.shape[0]):
        send[at] = (keep[at, 1 - row] + got[at, 1 - row].astype(f32)).astype(bf16)
        kept[at] = keep[at, row] + got[at, row].astype(f32)


def add(place_ref, keep, got, send, total):
    for at in range(keep.shape[0]):
        summed = keep[at] + got[at].astype(f32)
        total[at] = summed
        send[at] = summed.astype(bf16)


def window_kernel(place_ref, own_k, own_v, back_k, back_v, out_k, out_v):
    early = (place_ref[0] // 2) % 2 == 0

    @pl.when(early)
    def _():
        out_k[...] = own_k[...]
        out_v[...] = own_v[...]

    @pl.when(jnp.logical_not(early))
    def _():
        out_k[...] = back_k[...]
        out_v[...] = back_v[...]


def renorm_kernel(place_ref, old_ref, keep_p, got_p, keep_q, got_q, part_a, part_b):
    rows = part_a.shape[1]
    for at in range(3):
        keep, got = (keep_p[at], got_p[at]) if at < 2 else (keep_q[0], got_q[0])
        old = old_ref[at].astype(f32)
        updated = old + (keep + got.astype(f32))
        old_norm = jnp.sqrt(jnp.sum(old * old, axis=1, keepdims=True))
        squares = jnp.sum(updated * updated, axis=1, keepdims=True)
        fresh = updated * (old_norm / jnp.sqrt(squares + norm_eps))
        part_a[at] = fresh[:rows].astype(bf16)
        part_b[at] = fresh[rows:].astype(bf16)


def near_kernel(
    place_ref, part_a, got_a, part_b, got_b, own_k, own_v, back2_k, back2_v, back4_k, back4_v,
    near_a, near_b, near, pair,
):
    rows = part_a.shape[1]
    for at in range(3):
        for part, got, out, low in (
            (part_a, got_a, near_a, 0),
            (part_b, got_b, near_b, 2 * rows),
        ):
            both = jnp.concatenate([part[at].astype(f32), got[at].astype(f32)], axis=0)
            out[at] = both.astype(bf16)
            near[at, low : low + 2 * rows] = both.astype(bf16)
    even = place_ref[0] % 2 == 0

    @pl.when(even)
    def _():
        pair[0, 0] = own_k[...]
        pair[0, 1] = own_v[...]
        pair[1, 0] = back2_k[...]
        pair[1, 1] = back2_v[...]

    @pl.when(jnp.logical_not(even))
    def _():
        pair[0, 0] = back2_k[...]
        pair[0, 1] = back2_v[...]
        pair[1, 0] = back4_k[...]
        pair[1, 1] = back4_v[...]


def near_rows(place, part_a, got_a, part_b, got_b, blocks):
    rows, feats = part_a.shape[1:]
    return pl.pallas_call(
        near_kernel,
        out_shape=[
            jax.ShapeDtypeStruct((3, size * rows, feats), bf16) for size in (2, 2, 4)
        ]
        + [jax.ShapeDtypeStruct((2, 2) + blocks[0].shape, bf16)],
        in_specs=[SMEM] + [VMEM] * 10,
        out_specs=[VMEM] * 4,
        compiler_params=PARAMS,
        cost_estimate=cost(0, part_a.size * 14 + blocks[0].size * 8),
        name="near",
    )(place[None], part_a, got_a, part_b, got_b, *blocks)


def fast_output(query, hold):
    gate_q = lax.dot_general(
        query, hold[0], (((1,), (1,)), ((), ())), preferred_element_type=f32
    )
    up_q = lax.dot_general(query, hold[1], (((1,), (1,)), ((), ())), preferred_element_type=f32)
    hidden_q = (gate_q * jax.nn.sigmoid(gate_q) * up_q).astype(bf16)
    return jnp.dot(hidden_q, hold[2], preferred_element_type=f32)


def first_kernel(q_ref, near, near_other, out_ref, hold):
    rows = near.shape[1]
    hold[:, :rows] = near[...]
    hold[:, rows:] = near_other[...]
    out_ref[...] = fast_output(q_ref[...], hold)


def first_half(query, near, near_other):
    rows, feats = query.shape
    units = 2 * near.shape[1]
    return pl.pallas_call(
        first_kernel,
        out_shape=jax.ShapeDtypeStruct((rows, feats), f32),
        in_specs=[VMEM] * 3,
        out_specs=VMEM,
        scratch_shapes=[pltpu.VMEM((3, units, feats), bf16)],
        compiler_params=PARAMS,
        cost_estimate=cost(6 * rows * units * feats, 12 * units * feats, units * rows),
        name="first_half",
    )(query, near, near_other)


def far_kernel(got_a, got_b, attended, half_out, far, passed, passed_half):
    del attended, half_out, passed, passed_half
    rows = got_a.shape[1]
    far[:, :rows] = got_a[...]
    far[:, rows:] = got_b[...]


def far_rows(got_a, got_b, attended, half_out):
    shape = (3, 2 * got_a.shape[1], got_a.shape[2])
    return pl.pallas_call(
        far_kernel,
        out_shape=[
            jax.ShapeDtypeStruct(shape, bf16),
            jax.ShapeDtypeStruct(attended.shape, bf16),
            jax.ShapeDtypeStruct(half_out.shape, f32),
        ],
        in_specs=[VMEM] * 2 + [ANY] * 2,
        out_specs=[VMEM, ANY, ANY],
        input_output_aliases={2: 1, 3: 2},
        compiler_params=PARAMS,
        cost_estimate=cost(0, got_a.size * 8),
        name="far",
    )(got_a, got_b, attended, half_out)


def part_kernel(q_ref, before, rows_ref, out_ref):
    out_ref[...] = (before[...] + fast_output(q_ref[...], rows_ref)).astype(out_ref.dtype)


def part_step(query, before, weights, kind, name):
    rows, feats = query.shape
    units = weights.shape[1]
    return pl.pallas_call(
        part_kernel,
        out_shape=jax.ShapeDtypeStruct((rows, feats), kind),
        in_specs=[VMEM] * 3,
        out_specs=VMEM,
        compiler_params=PARAMS,
        cost_estimate=cost(6 * rows * units * feats, 6 * units * feats, units * rows),
        name=name,
    )(query, before, weights)


def body(att_q, att_k, att_v, fast_q, fast_k, fast_v, learn_rates, w_gate, w_up, w_down):
    count = lax.axis_size("seq")
    place = lax.axis_index("seq")
    feats, hidden = w_gate.shape
    quart = hidden // 8
    later = [1 << at for at in range(3, count.bit_length() - 1)]
    own_bit = {bit: (place // bit) % 2 for bit in [2, 4] + later}

    other_k, other_v = swapped(fast_k, 1), swapped(fast_v, 1)
    other_r = swapped(learn_rates, 1)
    turned_w = prepared(place, w_gate, w_up, w_down)
    send_p, send_q, keep_p, keep_q, own_k, own_v = gradients(
        place, turned_w, fast_k, other_k, fast_v, other_v,
        learn_rates[None, :], other_r[None, :], att_k, att_v,
    )
    around = [(at, (at + 4) % count) for at in range(count)]
    back4_k, back4_v = (lax.ppermute(part, "seq", around) for part in (own_k, own_v))
    rest = quart
    start = own_bit[2] * 2 * quart + own_bit[4] * quart
    for bit in later[:-1]:
        rest //= 2
        start += own_bit[bit] * rest
    old = lax.dynamic_slice_in_dim(turned_w, start, rest, 1)

    def shapes(matrices):
        return [((matrices, quart, feats), bf16), ((matrices, quart, feats), f32)]

    def scattered(send, total):
        for bit in later[:-1]:
            total = total.reshape(total.shape[0], 2, -1, feats)
            send = lax.dynamic_index_in_dim(total, 1 - own_bit[bit], 1, keepdims=False)
            total = lax.dynamic_index_in_dim(total, own_bit[bit], 1, keepdims=False)
            total = total + swapped(send.astype(bf16), bit).astype(f32)
            send = total.astype(bf16)
        return total, swapped(send, later[-1])

    got_p, got_q = swapped(send_p, 2), swapped(send_q, 2)
    send_p, keep_p = stage(halve, (place, keep_p, got_p), shapes(2), "second_p")
    got_p = swapped(send_p, 4)
    send_q, keep_q = stage(halve, (place, keep_q, got_q), shapes(1), "second_q", send_p)
    got_q = swapped(send_q, 4)
    send_p, total_p = stage(add, (place, keep_p, got_p), shapes(2), "third_p", send_q)
    windows = stage(
        window_kernel,
        (place, own_k, own_v, back4_k, back4_v),
        [(own_k.shape, bf16)] * 2,
        "window",
        send_p,
    )
    back2_k, back2_v = (swapped(part, 2) for part in windows)
    blocks = (own_k, own_v, back2_k, back2_v, back4_k, back4_v)
    total_p, got_p = scattered(send_p, total_p)
    send_q, total_q = stage(add, (place, keep_q, got_q), shapes(1), "third_q", send_p)
    total_q, got_q = scattered(send_q, total_q)
    part_a, part_b = stage(
        renorm_kernel,
        (place, old, total_p, got_p, total_q, got_q),
        [((3, rest // 2, feats), bf16)] * 2,
        "renorm",
    )

    for bit in reversed(later[:-1]):
        part_a = jnp.concatenate([part_a, swapped(part_a, bit)], axis=1)
        part_b = jnp.concatenate([part_b, swapped(part_b, bit)], axis=1)
    near_a, near_b, near, pair = near_rows(
        place, part_a, swapped(part_a, 4), part_b, swapped(part_b, 2), blocks
    )
    got_a, got_b = swapped(near_a, 2), swapped(near_b, 4)
    near_other = swapped(near, 1)
    pair = swapped(pair, 1)
    attended = attention(place, att_q, blocks, pair)
    half_out = first_half(fast_q, near, near_other)
    far, attended, half_out = far_rows(got_a, got_b, attended, half_out)
    half_out = part_step(fast_q, half_out, far, f32, "own_far")
    fast_out = part_step(fast_q, half_out, swapped(far, 1), bf16, "last")
    return (attended, fast_out)


def solution(mesh):
    tokens = P("seq", "head")
    weights = P(None, "head")
    return jax.shard_map(
        body,
        mesh=mesh,
        in_specs=(tokens,) * 6 + (P("seq"),) + (weights,) * 3,
        out_specs=(tokens, tokens),
        check_vma=False,
    )
```

time: 73.9 us -> 71.6 us (0.969)
  waiting for transfers between devices: 43.8 us -> 31.7 us
  starting transfers between devices: 12.7 us -> 19.8 us
  local copies, waits for them, and re-layouts: 2.3 us -> 5.12 us
    ppermute x14 -> x18, waiting for transfers between devices: 41.5 us -> 31.7 us  [swapped(): return lax.ppermute(value, 'seq', [(at, at ^ bit) for at in range(count)])]
    ppermute x14 -> x18, starting transfers between devices: 11.2 us -> 16.7 us  [swapped(): return lax.ppermute(value, 'seq', [(at, at ^ bit) for at in range(count)])]
    unnamed x16 -> x28, local copies, waits for them, and re-layouts: 1.31 us -> 5.09 us
    pallas_call x1, Pallas kernels: 3.03 us -> 0.57 us  [prepared(): pl.pallas_call(prepare_kernel, out_shape=jax.ShapeDtypeStruct((3, half, f...]
    ppermute x1 -> x2, waiting for transfers between devices: 2.3 us -> 0.01 us  [body(): lax.ppermute(part, 'seq', around)]
    pallas_call x6 -> x9, Pallas kernels: 5.25 us -> 7.51 us  [the longest x6 3.2 us: kernel_call(): pl.pallas_call(run, in_specs=list(in_specs) + [ANY] * len(tied), name=nam...]
    ppermute x1 -> x2, starting transfers between devices: 1.58 us -> 3.16 us  [body(): lax.ppermute(part, 'seq', around)]
    dynamic_slice x1, local copies, waits for them, and re-layouts: 0.99 us -> 0.03 us  [body(): old = lax.dynamic_slice_in_dim(turned_w, start, rest, 1)]
  transfers between devices with their start and end apart: 15 -> 20, of which waited for: 10 -> 11; matrix products, arithmetic and copies ran while one was open for 1% -> 0% of each run, Pallas kernels for 13% -> 14%
where the time goes in v1:
time: 71.6 us; the launch traced here: 71.3 us
  waiting for transfers between devices  31.7 us (44%)
  starting transfers between devices  19.8 us (28%)
  Pallas kernels  13.9 us (19%)
  local copies, waits for them, and re-layouts  5.12 us (7%)
  between operations  0.82 us (1%)
    ppermute x18, waiting for transfers between devices, swapped(): return lax.ppermute(value, 'seq', [(at, at ^ bit) for at in range(count)])  31.7 us
    ppermute x18, starting transfers between devices, swapped(): return lax.ppermute(value, 'seq', [(at, at ^ bit) for at in range(count)])  16.7 us
    unnamed x28, local copies, waits for them, and re-layouts  5.09 us
    pallas_call x1, Pallas kernels, attention(): pl.pallas_call(attention_kernel, out_shape=jax.ShapeDtypeStruct((rows, wi...  4.71 us
    pallas_call x6, Pallas kernels, kernel_call(): pl.pallas_call(run, in_specs=list(in_specs) + [ANY] * len(tied), name=nam...  3.2 us
    ppermute x2, starting transfers between devices, body(): lax.ppermute(part, 'seq', around)  3.16 us
    pallas_call x1, Pallas kernels, gradients(): pl.pallas_call(grad_kernel, out_shape=[jax.ShapeDtypeStruct((count, 2, ha...  2.4 us
    pallas_call x2, Pallas kernels, part_step(): pl.pallas_call(part_kernel, out_shape=jax.ShapeDtypeStruct((rows, feats),...  1.91 us
  transfers between devices with their start and end apart: 20, of which 11 were waited for; matrix products, arithmetic and copies ran while one was open for 0% of the time, Pallas kernels for 14%

profile of v1, /device:TPU:0, one launch (start us, length us, event | category | flops | bytes accessed | tf_op | source)
XLA Modules:
  0.0 71.3 jit_solution(11698197620274181734)
XLA Ops:
  0.6 0.5 collective-permute-start
  1.7 1.1 %copy-done.1 = bf16[640,640]{1,0:T(8,128)(2,1)S(1)} copy-done((bf16[640,640]{1,0:T(8,128)(2,1)S(1)}, bf16[640,640]{1,0:T(8,128)(2,1)}, u32[]{:S(2)}) %copy-start.1) | copy-done | bytes 819224
  2.8 1.1 %copy-done.2 = bf16[640,640]{1,0:T(8,128)(2,1)S(1)} copy-done((bf16[640,640]{1,0:T(8,128)(2,1)S(1)}, bf16[640,640]{1,0:T(8,128)(2,1)}, u32[]{:S(2)}) %copy-start.2) | copy-done | bytes 819224
  4.0 1.1 %copy-done.3 = bf16[640,640]{1,0:T(8,128)(2,1)S(1)} copy-done((bf16[640,640]{1,0:T(8,128)(2,1)S(1)}, bf16[640,640]{1,0:T(8,128)(2,1)}, u32[]{:S(2)}) %copy-start.3) | copy-done | bytes 819224
  5.1 0.6 prepare.1.turned_ref
  6.4 2.4 %gradients.1 = (bf16[2,2,80,640]{3,2,1,0:T(8,128)(2,1)S(1)}, bf16[1,2,80,640]{3,2,1,0:T(8,128)(2,1)S(1)}, f32[2,2,80,640]{3,2,1,0:T(8,128)S(1)}, f32[1,2,80,640]...) custom-call(s32[1]{0:T(128)} %bitcast.place_ref.refs_0_, ...), custom_call_target="tpu_custom_call" | custom-call | flops 1258291200 | bytes 4096000 | tf_op jit(solution)/shard_map/gradients/pallas_call | solution.py:180
  8.8 2.7 %collective-permute-start.3 = (bf16[2,2,80,640]{3,2,1,0:T(8,128)(2,1)S(1)}, bf16[2,2,80,640]{3,2,1,0:T(8,128)(2,1)S(1)}, u32[]{:S(2)}, u32[]{:S(2)}) collective-permute-start(bf16[2,2,80,640]{3,2,1,0:T(8,128)(2,1)S(1)} %get-tuple-element.28), channel_id=1, source_target_pairs={{0,4},{2,6},{4,0},{6,2},{8,12},{10,14},{12,8},{14,10},{16,20},{18,... | collective-permute-start | bytes 1228808 | tf_op jit(solution)/shard_map/ppermute | solution.py:26
  11.4 1.6 %collective-permute-start.11 = (bf16[256,640]{1,0:T(8,128)(2,1)S(1)}, bf16[256,640]{1,0:T(8,128)(2,1)S(1)}, u32[]{:S(2)}, u32[]{:S(2)}) collective-permute-start(bf16[256,640]{1,0:T(8,128)(2,1)S(1)} %get-tuple-element.41.refs_1_.own_k), channel_id=1, source_target_pairs={{0,8},{2,10},{4,12},{6,14},{8,16},{10,18},{12,20},{14,22},{16,24},... | collective-permute-start | bytes 983048 | tf_op jit(solution)/shard_map/ppermute | solution.py:388
  13.0 1.6 %collective-permute-start.12 = (bf16[256,640]{1,0:T(8,128)(2,1)S(1)}, bf16[256,640]{1,0:T(8,128)(2,1)S(1)}, u32[]{:S(2)}, u32[]{:S(2)}) collective-permute-start(bf16[256,640]{1,0:T(8,128)(2,1)S(1)} %get-tuple-element.42.refs_2_.own_v), channel_id=1, source_target_pairs={{0,8},{2,10},{4,12},{6,14},{8,16},{10,18},{12,20},{14,22},{16,24},... | collective-permute-start | bytes 983048 | tf_op jit(solution)/shard_map/ppermute | solution.py:388
  14.6 0.5 collective-permute-start.5
  15.1 6.7 %collective-permute-done.3.refs_2_ = bf16[2,2,80,640]{3,2,1,0:T(8,128)(2,1)S(1)} collective-permute-done((bf16[2,2,80,640]{3,2,1,0:T(8,128)(2,1)S(1)}, bf16[2,2,80,640]{3,2,1,0:T(8,128)(2,1)S(1)}, u32[]{:S(2)}, u32[]{:S(2)}) %collective-permute-start.3) | collective-permute-done | bytes 409632 | tf_op jit(solution)/shard_map/ppermute | solution.py:26
  21.8 2.1 %collective-permute-start.4 = (bf16[2,80,640]{2,1,0:T(8,128)(2,1)S(1)}, bf16[2,80,640]{2,1,0:T(8,128)(2,1)S(1)}, u32[]{:S(2)}, u32[]{:S(2)}) collective-permute-start(bf16[2,80,640]{2,1,0:T(8,128)(2,1)S(1)} %get-tuple-element.30.refs_3_), channel_id=1, source_target_pairs={{0,8},{2,10},{4,12},{6,14},{8,0},{10,2},{12,4},{14,6},{16,24},{18,... | collective-permute-start | bytes 614408 | tf_op jit(solution)/shard_map/ppermute | solution.py:26
  23.9 2.0 %collective-permute-done.5.refs_2_ = bf16[1,2,80,640]{3,2,1,0:T(8,128)(2,1)S(1)} collective-permute-done((bf16[1,2,80,640]{3,2,1,0:T(8,128)(2,1)S(1)}, bf16[1,2,80,640]{3,2,1,0:T(8,128)(2,1)S(1)}, u32[]{:S(2)}, u32[]{:S(2)}) %collective-permute-start.5) | collective-permute-done | bytes 204832 | tf_op jit(solution)/shard_map/ppermute | solution.py:26
  25.9 1.9 %collective-permute-start.7 = (bf16[1,80,640]{2,1,0:T(8,128)(2,1)S(1)}, bf16[1,80,640]{2,1,0:T(8,128)(2,1)}, u32[]{:S(2)}, u32[]{:S(2)}) collective-permute-start(bf16[1,80,640]{2,1,0:T(8,128)(2,1)S(1)} %get-tuple-element.33.refs_3_), channel_id=1, source_target_pairs={{0,8},{2,10},{4,12},{6,14},{8,0},{10,2},{12,4},{14,6},{16,24},{18,... | collective-permute-start | bytes 307208 | tf_op jit(solution)/shard_map/ppermute | solution.py:26
  27.8 6.8 %collective-permute-done.4.refs_2_ = bf16[2,80,640]{2,1,0:T(8,128)(2,1)S(1)} collective-permute-done((bf16[2,80,640]{2,1,0:T(8,128)(2,1)S(1)}, bf16[2,80,640]{2,1,0:T(8,128)(2,1)S(1)}, u32[]{:S(2)}, u32[]{:S(2)}) %collective-permute-start.4) | collective-permute-done | bytes 204832 | tf_op jit(solution)/shard_map/ppermute | solution.py:26
  34.6 1.2 %collective-permute-start.6 = (bf16[2,80,640]{2,1,0:T(8,128)(2,1)S(1)}, bf16[2,80,640]{2,1,0:T(8,128)(2,1)}, u32[]{:S(2)}, u32[]{:S(2)}) collective-permute-start(bf16[2,80,640]{2,1,0:T(8,128)(2,1)S(1)} %get-tuple-element.35.refs_3_.refs_5_), channel_id=1, source_target_pairs={{0,16},{2,18},{4,20},{6,22},{8,24},{10,26},{12,28},{14,30},{16,0},... | collective-permute-start | bytes 614408 | tf_op jit(solution)/shard_map/ppermute | solution.py:26
  35.9 0.9 %window.1 = (bf16[256,640]{1,0:T(8,128)(2,1)}, bf16[256,640]{1,0:T(8,128)(2,1)}) custom-call(s32[1]{0:T(128)} %bitcast.place_ref.refs_0_, bf16[256,640]{1,0:T(8,128)(2,1)S(1)} %get-tuple-element.41.refs_1_.own_k, bf16[256,640]{1,0:T(8,128)(2,1)S(1)} %get-tuple-element.42.refs_2_.own_v, bf16[256,640]{1,0:T(8,128)(2,1)S(1)} %collective-permute-done.11.refs_3_.back4_k, ...), custom_call_target="tpu_custom_call" | custom-call | tf_op jit(solution)/shard_map/window/pallas_call | solution.py:35
  37.0 1.8 %collective-permute-start.14 = (bf16[256,640]{1,0:T(8,128)(2,1)}, bf16[256,640]{1,0:T(8,128)(2,1)S(1)}, u32[]{:S(2)}, u32[]{:S(2)}) collective-permute-start(bf16[256,640]{1,0:T(8,128)(2,1)} %get-tuple-element.44), channel_id=1, source_target_pairs={{0,4},{2,6},{4,0},{6,2},{8,12},{10,14},{12,8},{14,10},{16,20},{18,... | collective-permute-start | bytes 983048 | tf_op jit(solution)/shard_map/ppermute | solution.py:26
  38.8 1.0 %copy-done.8 = f32[1,80,640]{2,1,0:T(8,128)S(1)} copy-done((f32[1,80,640]{2,1,0:T(8,128)S(1)}, f32[1,80,640]{2,1,0:T(8,128)}, u32[]{:S(2)}) %copy-start.8) | copy-done | bytes 204824
  39.8 0.9 %third_q.1 = (bf16[1,80,640]{2,1,0:T(8,128)(2,1)S(1)}, f32[1,80,640]{2,1,0:T(8,128)S(1)}) custom-call(s32[1]{0:T(128)} %bitcast.place_ref.refs_0_, f32[1,80,640]{2,1,0:T(8,128)S(1)} %copy-done.8, bf16[1,80,640]{2,1,0:T(8,128)(2,1)} %collective-permute-done.7.refs_2_, bf16[2,80,640]{2,1,0:T(8,128)(2,1)S(1)} %get-tuple-element.35.refs_3_.refs_5_), custom_call_target="tpu_custom_call" | custom-call | tf_op jit(solution)/shard_map/third_q/pallas_call | solution.py:35
  40.7 1.8 %collective-permute-start.8 = (bf16[1,80,640]{2,1,0:T(8,128)(2,1)S(1)}, bf16[1,80,640]{2,1,0:T(8,128)(2,1)S(1)}, u32[]{:S(2)}, u32[]{:S(2)}) collective-permute-start(bf16[1,80,640]{2,1,0:T(8,128)(2,1)S(1)} %get-tuple-element.38), channel_id=1, source_target_pairs={{0,16},{2,18},{4,20},{6,22},{8,24},{10,26},{12,28},{14,30},{16,0},... | collective-permute-start | bytes 307208 | tf_op jit(solution)/shard_map/ppermute | solution.py:26
  42.6 7.7 %collective-permute-done.8.refs_5_ = bf16[1,80,640]{2,1,0:T(8,128)(2,1)S(1)} collective-permute-done((bf16[1,80,640]{2,1,0:T(8,128)(2,1)S(1)}, bf16[1,80,640]{2,1,0:T(8,128)(2,1)S(1)}, u32[]{:S(2)}, u32[]{:S(2)}) %collective-permute-start.8) | collective-permute-done | bytes 102432 | tf_op jit(solution)/shard_map/ppermute | solution.py:26
  50.3 1.2 %renorm.1 = (bf16[3,40,640]{2,1,0:T(8,128)(2,1)S(1)}, bf16[3,40,640]{2,1,0:T(8,128)(2,1)S(1)}) custom-call(s32[1]{0:T(128)} %bitcast.place_ref.refs_0_, bf16[3,80,640]{2,1,0:T(8,128)(2,1)S(1)} %constant_dynamic-slice_fusion.refs_1_, f32[2,80,640]{2,1,0:T(8,128)S(1)} %copy-done.5, bf16[2,80,640]{2,1,0:T(8,128)(2,1)} %collective-permute-done.6.refs_3_, ...), custom_call_target="tpu_custom_call" | custom-call | tf_op jit(solution)/shard_map/renorm/pallas_call | solution.py:35
  51.6 0.6 collective-permute-start.10
  52.4 5.0 %collective-permute-done.9.got_a = bf16[3,40,640]{2,1,0:T(8,128)(2,1)S(1)} collective-permute-done((bf16[3,40,640]{2,1,0:T(8,128)(2,1)S(1)}, bf16[3,40,640]{2,1,0:T(8,128)(2,1)S(1)}, u32[]{:S(2)}, u32[]{:S(2)}) %collective-permute-start.9) | collective-permute-done | bytes 153632 | tf_op jit(solution)/shard_map/ppermute | solution.py:26
  58.8 1.7 %collective-permute-start.16 = (bf16[3,80,640]{2,1,0:T(8,128)(2,1)S(1)}, bf16[3,80,640]{2,1,0:T(8,128)(2,1)S(1)}, u32[]{:S(2)}, u32[]{:S(2)}) collective-permute-start(bf16[3,80,640]{2,1,0:T(8,128)(2,1)S(1)} %get-tuple-element.46), channel_id=1, source_target_pairs={{0,8},{2,10},{4,12},{6,14},{8,0},{10,2},{12,4},{14,6},{16,24},{18,... | collective-permute-start | bytes 921608 | tf_op jit(solution)/shard_map/ppermute | solution.py:26
  60.5 1.2 %collective-permute-done.18.near_other = bf16[3,160,640]{2,1,0:T(8,128)(2,1)S(1)} collective-permute-done((bf16[3,160,640]{2,1,0:T(8,128)(2,1)S(1)}, bf16[3,160,640]{2,1,0:T(8,128)(2,1)S(1)}, u32[]{:S(2)}, u32[]{:S(2)}) %collective-permute-start.18) | collective-permute-done | bytes 614432 | tf_op jit(solution)/shard_map/ppermute | solution.py:26
  61.7 0.8 %first_half.1.half_out = f32[256,640]{1,0:T(8,128)S(1)} custom-call(bf16[256,640]{1,0:T(8,128)(2,1)S(1)} %copy-done, bf16[3,160,640]{2,1,0:T(8,128)(2,1)S(1)} %get-tuple-element.48.near, bf16[3,160,640]{2,1,0:T(8,128)(2,1)S(1)} %collective-permute-done.18.near_other), custom_call_target="tpu_custom_call" | custom-call | flops 314572800 | bytes 2457600 | tf_op jit(solution)/shard_map/first_half/pallas_call | solution.py:317
  62.6 4.7 %attention.1.attended = bf16[256,640]{1,0:T(8,128)(2,1)} custom-call(s32[1]{0:T(128)} %bitcast.place_ref.refs_0_, bf16[256,640]{1,0:T(8,128)(2,1)S(1)} %copy-done.6, bf16[256,640]{1,0:T(8,128)(2,1)S(1)} %get-tuple-element.41.refs_1_.own_k, bf16[256,640]{1,0:T(8,128)(2,1)S(1)} %get-tuple-element.42.refs_2_.own_v, ...), custom_call_target="tpu_custom_call" | custom-call | flops 838860800 | bytes 3932160 | tf_op jit(solution)/shard_map/attention/pallas_call | solution.py:94
  67.9 0.6 own_far.1.before
  68.5 1.4 %collective-permute-done.19.rows_ref = bf16[3,160,640]{2,1,0:T(8,128)(2,1)S(1)} collective-permute-done((bf16[3,160,640]{2,1,0:T(8,128)(2,1)S(1)}, bf16[3,160,640]{2,1,0:T(8,128)(2,1)S(1)}, u32[]{:S(2)}, u32[]{:S(2)}) %collective-permute-start.19) | collective-permute-done | bytes 614432 | tf_op jit(solution)/shard_map/ppermute | solution.py:26
  70.0 1.3 %last.1 = bf16[256,640]{1,0:T(8,128)(2,1)} custom-call(bf16[256,640]{1,0:T(8,128)(2,1)S(1)} %copy-done, f32[256,640]{1,0:T(8,128)S(1)} %own_far.1.before, bf16[3,160,640]{2,1,0:T(8,128)(2,1)S(1)} %collective-permute-done.19.rows_ref), custom_call_target="tpu_custom_call" | custom-call | flops 157286400 | bytes 614400 | tf_op jit(solution)/shard_map/last/pallas_call | solution.py:361
  (51 shorter events, 4.0 us)
Async XLA Ops:
  0.6 5.1 %collective-permute-start = (bf16[256,640]{1,0:T(8,128)(2,1)}, bf16[256,640]{1,0:T(8,128)(2,1)S(1)}, u32[]{:S(2)}, u32[]{:S(2)}) collective-permute-start(bf16[256,640]{1,0:T(8,128)(2,1)} %k0_ref.1), channel_id=1, source_target_pairs={{0,2},{2,0},{4,6},{6,4},{8,10},{10,8},{12,14},{14,12},{16,18},{18,... | collective-permute-start | bytes 983048 | tf_op jit(solution)/shard_map/ppermute | solution.py:26
  1.2 4.6 %collective-permute-start.1 = (bf16[256,640]{1,0:T(8,128)(2,1)}, bf16[256,640]{1,0:T(8,128)(2,1)S(1)}, u32[]{:S(2)}, u32[]{:S(2)}) collective-permute-start(bf16[256,640]{1,0:T(8,128)(2,1)} %v0_ref.1), channel_id=1, source_target_pairs={{0,2},{2,0},{4,6},{6,4},{8,10},{10,8},{12,14},{14,12},{16,18},{18,... | collective-permute-start | bytes 983048 | tf_op jit(solution)/shard_map/ppermute | solution.py:26
  1.2 4.5 %collective-permute-start.2 = (f32[256]{0:T(256)}, f32[256]{0:T(256)S(1)}, u32[]{:S(2)}, u32[]{:S(2)}) collective-permute-start(f32[256]{0:T(256)} %param.16), channel_id=1, source_target_pairs={{0,2},{2,0},{4,6},{6,4},{8,10},{10,8},{12,14},{14,12},{16,18},{18,... | collective-permute-start | bytes 3080 | tf_op jit(solution)/shard_map/ppermute | solution.py:26
  1.7 1.1 %copy-start.1 = (bf16[640,640]{1,0:T(8,128)(2,1)S(1)}, bf16[640,640]{1,0:T(8,128)(2,1)}, u32[]{:S(2)}) copy-start(bf16[640,640]{1,0:T(8,128)(2,1)} %gate_ref.1) | copy-start | bytes 2457604
  2.8 1.1 %copy-start.2 = (bf16[640,640]{1,0:T(8,128)(2,1)S(1)}, bf16[640,640]{1,0:T(8,128)(2,1)}, u32[]{:S(2)}) copy-start(bf16[640,640]{1,0:T(8,128)(2,1)} %up_ref.1) | copy-start | bytes 2457604
  4.0 1.1 %copy-start.3 = (bf16[640,640]{1,0:T(8,128)(2,1)S(1)}, bf16[640,640]{1,0:T(8,128)(2,1)}, u32[]{:S(2)}) copy-start(bf16[640,640]{1,0:T(8,128)(2,1)} %down_ref.1) | copy-start | bytes 2457604
  5.1 1.1 %copy-start.10 = (bf16[256,640]{1,0:T(8,128)(2,1)S(1)}, bf16[256,640]{1,0:T(8,128)(2,1)}, u32[]{:S(2)}) copy-start(bf16[256,640]{1,0:T(8,128)(2,1)} %v0_ref.1) | copy-start | bytes 983044
  5.1 1.2 %copy-start.11 = (bf16[256,640]{1,0:T(8,128)(2,1)S(1)}, bf16[256,640]{1,0:T(8,128)(2,1)}, u32[]{:S(2)}) copy-start(bf16[256,640]{1,0:T(8,128)(2,1)} %key_ref.1) | copy-start | bytes 983044
  5.1 1.3 %copy-start.12 = (bf16[256,640]{1,0:T(8,128)(2,1)S(1)}, bf16[256,640]{1,0:T(8,128)(2,1)}, u32[]{:S(2)}) copy-start(bf16[256,640]{1,0:T(8,128)(2,1)} %val_ref.1) | copy-start | bytes 983044
  5.1 1.3 %copy-start.13 = (f32[256]{0:T(256)S(1)}, f32[256]{0:T(256)}, u32[]{:S(2)}) copy-start(f32[256]{0:T(256)} %param.16) | copy-start | bytes 3076
  8.8 13.0 %collective-permute-start.3 = (bf16[2,2,80,640]{3,2,1,0:T(8,128)(2,1)S(1)}, bf16[2,2,80,640]{3,2,1,0:T(8,128)(2,1)S(1)}, u32[]{:S(2)}, u32[]{:S(2)}) collective-permute-start(bf16[2,2,80,640]{3,2,1,0:T(8,128)(2,1)S(1)} %get-tuple-element.28), channel_id=1, source_target_pairs={{0,4},{2,6},{4,0},{6,2},{8,12},{10,14},{12,8},{14,10},{16,20},{18,... | collective-permute-start | bytes 1228808 | tf_op jit(solution)/shard_map/ppermute | solution.py:26
  11.4 24.4 %collective-permute-start.11 = (bf16[256,640]{1,0:T(8,128)(2,1)S(1)}, bf16[256,640]{1,0:T(8,128)(2,1)S(1)}, u32[]{:S(2)}, u32[]{:S(2)}) collective-permute-start(bf16[256,640]{1,0:T(8,128)(2,1)S(1)} %get-tuple-element.41.refs_1_.own_k), channel_id=1, source_target_pairs={{0,8},{2,10},{4,12},{6,14},{8,16},{10,18},{12,20},{14,22},{16,24},... | collective-permute-start | bytes 983048 | tf_op jit(solution)/shard_map/ppermute | solution.py:388
  13.0 22.9 %collective-permute-start.12 = (bf16[256,640]{1,0:T(8,128)(2,1)S(1)}, bf16[256,640]{1,0:T(8,128)(2,1)S(1)}, u32[]{:S(2)}, u32[]{:S(2)}) collective-permute-start(bf16[256,640]{1,0:T(8,128)(2,1)S(1)} %get-tuple-element.42.refs_2_.own_v), channel_id=1, source_target_pairs={{0,8},{2,10},{4,12},{6,14},{8,16},{10,18},{12,20},{14,22},{16,24},... | collective-permute-start | bytes 983048 | tf_op jit(solution)/shard_map/ppermute | solution.py:388
  14.6 11.3 %collective-permute-start.5 = (bf16[1,2,80,640]{3,2,1,0:T(8,128)(2,1)S(1)}, bf16[1,2,80,640]{3,2,1,0:T(8,128)(2,1)S(1)}, u32[]{:S(2)}, u32[]{:S(2)}) collective-permute-start(bf16[1,2,80,640]{3,2,1,0:T(8,128)(2,1)S(1)} %get-tuple-element.32), channel_id=1, source_target_pairs={{0,4},{2,6},{4,0},{6,2},{8,12},{10,14},{12,8},{14,10},{16,20},{18,... | collective-permute-start | bytes 614408 | tf_op jit(solution)/shard_map/ppermute | solution.py:26
  21.8 12.7 %collective-permute-start.4 = (bf16[2,80,640]{2,1,0:T(8,128)(2,1)S(1)}, bf16[2,80,640]{2,1,0:T(8,128)(2,1)S(1)}, u32[]{:S(2)}, u32[]{:S(2)}) collective-permute-start(bf16[2,80,640]{2,1,0:T(8,128)(2,1)S(1)} %get-tuple-element.30.refs_3_), channel_id=1, source_target_pairs={{0,8},{2,10},{4,12},{6,14},{8,0},{10,2},{12,4},{14,6},{16,24},{18,... | collective-permute-start | bytes 614408 | tf_op jit(solution)/shard_map/ppermute | solution.py:26
  25.9 11.1 %copy-start.7 = (f32[1,80,640]{2,1,0:T(8,128)}, f32[1,80,640]{2,1,0:T(8,128)S(1)}, u32[]{:S(2)}) copy-start(f32[1,80,640]{2,1,0:T(8,128)S(1)} %get-tuple-element.36.refs_1_) | copy-start | bytes 614404
  25.9 12.9 %collective-permute-start.7 = (bf16[1,80,640]{2,1,0:T(8,128)(2,1)S(1)}, bf16[1,80,640]{2,1,0:T(8,128)(2,1)}, u32[]{:S(2)}, u32[]{:S(2)}) collective-permute-start(bf16[1,80,640]{2,1,0:T(8,128)(2,1)S(1)} %get-tuple-element.33.refs_3_), channel_id=1, source_target_pairs={{0,8},{2,10},{4,12},{6,14},{8,0},{10,2},{12,4},{14,6},{16,24},{18,... | collective-permute-start | bytes 307208 | tf_op jit(solution)/shard_map/ppermute | solution.py:26
  34.6 2.1 %copy-start.4 = (f32[2,80,640]{2,1,0:T(8,128)}, f32[2,80,640]{2,1,0:T(8,128)S(1)}, u32[]{:S(2)}) copy-start(f32[2,80,640]{2,1,0:T(8,128)S(1)} %get-tuple-element.34.refs_2_) | copy-start | bytes 1228804
  34.6 15.6 %collective-permute-start.6 = (bf16[2,80,640]{2,1,0:T(8,128)(2,1)S(1)}, bf16[2,80,640]{2,1,0:T(8,128)(2,1)}, u32[]{:S(2)}, u32[]{:S(2)}) collective-permute-start(bf16[2,80,640]{2,1,0:T(8,128)(2,1)S(1)} %get-tuple-element.35.refs_3_.refs_5_), channel_id=1, source_target_pairs={{0,16},{2,18},{4,20},{6,22},{8,24},{10,26},{12,28},{14,30},{16,0},... | collective-permute-start | bytes 614408 | tf_op jit(solution)/shard_map/ppermute | solution.py:26
  36.8 15.4 %collective-permute-start.13 = (bf16[256,640]{1,0:T(8,128)(2,1)}, bf16[256,640]{1,0:T(8,128)(2,1)S(1)}, u32[]{:S(2)}, u32[]{:S(2)}) collective-permute-start(bf16[256,640]{1,0:T(8,128)(2,1)} %get-tuple-element.43), channel_id=1, source_target_pairs={{0,4},{2,6},{4,0},{6,2},{8,12},{10,14},{12,8},{14,10},{16,20},{18,... | collective-permute-start | bytes 983048 | tf_op jit(solution)/shard_map/ppermute | solution.py:26
  37.0 15.4 %collective-permute-start.14 = (bf16[256,640]{1,0:T(8,128)(2,1)}, bf16[256,640]{1,0:T(8,128)(2,1)S(1)}, u32[]{:S(2)}, u32[]{:S(2)}) collective-permute-start(bf16[256,640]{1,0:T(8,128)(2,1)} %get-tuple-element.44), channel_id=1, source_target_pairs={{0,4},{2,6},{4,0},{6,2},{8,12},{10,14},{12,8},{14,10},{16,20},{18,... | collective-permute-start | bytes 983048 | tf_op jit(solution)/shard_map/ppermute | solution.py:26
  38.8 11.5 %copy-start.5 = (f32[2,80,640]{2,1,0:T(8,128)S(1)}, f32[2,80,640]{2,1,0:T(8,128)}, u32[]{:S(2)}) copy-start(f32[2,80,640]{2,1,0:T(8,128)} %copy-done.4) | copy-start | bytes 1228804
  40.7 9.5 %collective-permute-start.8 = (bf16[1,80,640]{2,1,0:T(8,128)(2,1)S(1)}, bf16[1,80,640]{2,1,0:T(8,128)(2,1)S(1)}, u32[]{:S(2)}, u32[]{:S(2)}) collective-permute-start(bf16[1,80,640]{2,1,0:T(8,128)(2,1)S(1)} %get-tuple-element.38), channel_id=1, source_target_pairs={{0,16},{2,18},{4,20},{6,22},{8,24},{10,26},{12,28},{14,30},{16,0},... | collective-permute-start | bytes 307208 | tf_op jit(solution)/shard_map/ppermute | solution.py:26
  51.5 10.3 %copy-start = (bf16[256,640]{1,0:T(8,128)(2,1)S(1)}, bf16[256,640]{1,0:T(8,128)(2,1)}, u32[]{:S(2)}) copy-start(bf16[256,640]{1,0:T(8,128)(2,1)} %q_ref.7) | copy-start | bytes 983044
  51.5 6.0 %collective-permute-start.9 = (bf16[3,40,640]{2,1,0:T(8,128)(2,1)S(1)}, bf16[3,40,640]{2,1,0:T(8,128)(2,1)S(1)}, u32[]{:S(2)}, u32[]{:S(2)}) collective-permute-start(bf16[3,40,640]{2,1,0:T(8,128)(2,1)S(1)} %get-tuple-element.39.part_a), channel_id=1, source_target_pairs={{0,8},{2,10},{4,12},{6,14},{8,0},{10,2},{12,4},{14,6},{16,24},{18,... | collective-permute-start | bytes 460808 | tf_op jit(solution)/shard_map/ppermute | solution.py:26
  51.6 6.0 %collective-permute-start.10 = (bf16[3,40,640]{2,1,0:T(8,128)(2,1)S(1)}, bf16[3,40,640]{2,1,0:T(8,128)(2,1)S(1)}, u32[]{:S(2)}, u32[]{:S(2)}) collective-permute-start(bf16[3,40,640]{2,1,0:T(8,128)(2,1)S(1)} %get-tuple-element.40.part_b), channel_id=1, source_target_pairs={{0,4},{2,6},{4,0},{6,2},{8,12},{10,14},{12,8},{14,10},{16,20},{18,... | collective-permute-start | bytes 460808 | tf_op jit(solution)/shard_map/ppermute | solution.py:26
  57.8 4.8 %copy-start.6 = (bf16[256,640]{1,0:T(8,128)(2,1)S(1)}, bf16[256,640]{1,0:T(8,128)(2,1)}, u32[]{:S(2)}) copy-start(bf16[256,640]{1,0:T(8,128)(2,1)} %q_ref.4) | copy-start | bytes 983044
  57.8 4.8 %collective-permute-start.17 = (bf16[2,2,256,640]{3,2,1,0:T(8,128)(2,1)S(1)}, bf16[2,2,256,640]{3,2,1,0:T(8,128)(2,1)S(1)}, u32[]{:S(2)}, u32[]{:S(2)}) collective-permute-start(bf16[2,2,256,640]{3,2,1,0:T(8,128)(2,1)S(1)} %get-tuple-element.47), channel_id=1, source_target_pairs={{0,2},{2,0},{4,6},{6,4},{8,10},{10,8},{12,14},{14,12},{16,18},{18,... | collective-permute-start | bytes 3932168 | tf_op jit(solution)/shard_map/ppermute | solution.py:26
  57.8 3.9 %collective-permute-start.18 = (bf16[3,160,640]{2,1,0:T(8,128)(2,1)S(1)}, bf16[3,160,640]{2,1,0:T(8,128)(2,1)S(1)}, u32[]{:S(2)}, u32[]{:S(2)}) collective-permute-start(bf16[3,160,640]{2,1,0:T(8,128)(2,1)S(1)} %get-tuple-element.48.near), channel_id=1, source_target_pairs={{0,2},{2,0},{4,6},{6,4},{8,10},{10,8},{12,14},{14,12},{16,18},{18,... | collective-permute-start | bytes 1843208 | tf_op jit(solution)/shard_map/ppermute | solution.py:26
  58.3 9.3 %collective-permute-start.15 = (bf16[3,80,640]{2,1,0:T(8,128)(2,1)S(1)}, bf16[3,80,640]{2,1,0:T(8,128)(2,1)S(1)}, u32[]{:S(2)}, u32[]{:S(2)}) collective-permute-start(bf16[3,80,640]{2,1,0:T(8,128)(2,1)S(1)} %get-tuple-element.45), channel_id=1, source_target_pairs={{0,4},{2,6},{4,0},{6,2},{8,12},{10,14},{12,8},{14,10},{16,20},{18,... | collective-permute-start | bytes 921608 | tf_op jit(solution)/shard_map/ppermute | solution.py:26
  58.8 9.0 %collective-permute-start.16 = (bf16[3,80,640]{2,1,0:T(8,128)(2,1)S(1)}, bf16[3,80,640]{2,1,0:T(8,128)(2,1)S(1)}, u32[]{:S(2)}, u32[]{:S(2)}) collective-permute-start(bf16[3,80,640]{2,1,0:T(8,128)(2,1)S(1)} %get-tuple-element.46), channel_id=1, source_target_pairs={{0,8},{2,10},{4,12},{6,14},{8,0},{10,2},{12,4},{14,6},{16,24},{18,... | collective-permute-start | bytes 921608 | tf_op jit(solution)/shard_map/ppermute | solution.py:26
  67.9 2.1 %collective-permute-start.19 = (bf16[3,160,640]{2,1,0:T(8,128)(2,1)S(1)}, bf16[3,160,640]{2,1,0:T(8,128)(2,1)S(1)}, u32[]{:S(2)}, u32[]{:S(2)}) collective-permute-start(bf16[3,160,640]{2,1,0:T(8,128)(2,1)S(1)} %get-tuple-element.51.rows_ref), channel_id=1, source_target_pairs={{0,2},{2,0},{4,6},{6,4},{8,10},{10,8},{12,14},{14,12},{16,18},{18,... | collective-permute-start | bytes 1843208 | tf_op jit(solution)/shard_map/ppermute | solution.py:26
  (2 other events, 2.0 us)
